TPU v7x, 32 devices: a whole 2x2x4 slice. The times are simulated.
32 devices in a mesh: seq: 8 (over z, y), head: 2 (over x), batch: 2 (over core).
Axes of the slice: x: 2, y: 2, z: 4, core: 2. Of those that a mesh axis runs over, the one named last changes fastest.
Arguments:
- tokens: float32 [2, 8192, 1024], P('batch', ('seq', 'head')), may hold values from -6 to 6
- cotangent: float32 [2, 8192, 1024], P('batch', ('seq', 'head')), may hold values from -6 to 6
- doc_lengths: int32 [2, 8], P('batch'), may hold values from 0 to 8192, as said below
- adapter_ids: int32 [2], P('batch'), may hold values from 0 to 7
- query_weight: bfloat16 [1024, 1024], replicated, may hold values from -0.25 to 0.25
- key_weight: bfloat16 [1024, 1024], replicated, may hold values from -0.25 to 0.25
- value_weight: bfloat16 [1024, 1024], replicated, may hold values from -0.1875 to 0.1875
- output_weight: bfloat16 [1024, 1024], replicated, may hold values from -0.75 to 0.75
- up_weight: bfloat16 [1024, 4096], replicated, may hold values from -0.1875 to 0.1875
- down_weight: bfloat16 [4096, 1024], replicated, may hold values from -0.09375 to 0.09375
- attention_gain: float32 [1024], replicated, may hold values from 0.1 to 1.9
- feedforward_gain: float32 [1024], replicated, may hold values from 0.1 to 1.9
- position_gain: float32 [1024], replicated, may hold values from 0.1 to 1.9
- position_table: float32 [512, 1024], replicated, may hold values from -6 to 6
- attention_down: float32 [4, 8, 1024, 16], replicated, may hold values from -0.1875 to 0.1875
- attention_up: float32 [4, 8, 16, 1024], replicated, may hold values from -0.375 to 0.375
- expand_down: float32 [8, 1024, 16], replicated, may hold values from -0.1875 to 0.1875
- expand_up: float32 [8, 16, 4096], replicated, may hold values from -0.375 to 0.375
- reduce_down: float32 [8, 4096, 16], replicated, may hold values from -0.09375 to 0.09375
- reduce_up: float32 [8, 16, 1024], replicated, may hold values from -0.375 to 0.375
Outputs:
- layer_output: float32 [2, 8192, 1024], P('batch', ('seq', 'head'))
- input_grad: float32 [2, 8192, 1024], P('batch', ('seq', 'head'))
- table_grad: float32 [512, 1024], P('head')
- attention_down_grad: float32 [4, 8, 1024, 16], P(None, 'head')
- attention_up_grad: float32 [4, 8, 16, 1024], P(None, 'head')
- expand_down_grad: float32 [8, 1024, 16], P('head')
- expand_up_grad: float32 [8, 16, 4096], P('head')
- reduce_down_grad: float32 [8, 4096, 16], P('head')
- reduce_up_grad: float32 [8, 16, 1024], P('head')
Inputs may be any that keep to these rules, and one draw needn't show every extreme that they name: `doc_lengths`: each row holds 8 document lengths whose sum is at most 8192; positions past the sum are padding. In each group of 1 row one row, drawn from the seed, holds a first document that ends within the last block of positions of one device (in the first group at the sequence's last position, so that it is 8192 long), then a second document of at most the remaining positions (possibly empty), then zeros; every other row holds lengths from 512 to 1024.
All inputs are finite; a program needn't handle non-finite values.
Results may differ from a plain program's by a relative error of at most 0.015.
The roundings to bfloat16 on the way count: a program that leaves them out, or rounds other values in their place, can miss the bound.
Values may be sent and summed in bfloat16 or wider, within the bound.
A program may use at most 704 MiB of HBM per device.

v0:
```python
from functools import partial
import math

import jax
import jax.numpy as jnp
import numpy as np
from jax import lax
from jax.sharding import PartitionSpec as P

HEADS = 16
HEAD_DIM = 64
BUCK = 256
SPAN = 512
ADAPTERS = 8
HALF = 512
DOCS = 8


EPSILON = 1e-07
ADAPTER_SCALING = 2.0
NEGATIVE = -1e30
PRECISE = lax.Precision.HIGHEST


def with_halo(cells, sides, width):
    for axis, dim in sides:
        count = lax.axis_size(axis)
        ends = count - 1
        head = lax.slice_in_dim(cells, 0, width, axis=dim)
        tail = lax.slice_in_dim(cells, cells.shape[dim] - width, cells.shape[dim], axis=dim)
        cells = jnp.concatenate(
            [
                lax.ppermute(tail, axis, [(i, (i + 1) % count) for i in range(ends)]),
                cells,
                lax.ppermute(head, axis, [((i + 1) % count, i) for i in range(ends)]),
            ],
            axis=dim,
        )
    return cells


def for_sending(array):

    def short(part):
        return part.astype(jnp.bfloat16) if part.dtype == jnp.float32 else part

    return jax.tree.map(short, array)


def shifted(value, axis, steps):
    count = lax.axis_size(axis)
    initial, last = (max(0, -steps), min(count, count - steps))
    return lax.ppermute(value, axis, [(source, source + steps) for source in range(initial, last)])


def bucket_of(offset, buckets, distance_cap):
    middle = buckets // 2
    sign_of = np.sign(offset)
    magnitude = np.where((offset < middle) & (offset > -middle), middle - 1, np.abs(offset))
    log_place = (
        np.ceil(np.log(magnitude / middle) / np.log((distance_cap - 1) / middle) * (middle - 1))
        + middle
    )
    return np.where(np.abs(offset) <= middle, offset, log_place * sign_of).astype(np.int32)


def relative_tables(half_span, buckets, distance_cap):
    places = np.arange(2 * half_span)
    key_side = np.clip(half_span - places, 1 - half_span, half_span - 1)
    query_side = np.clip(places - half_span, 1 - half_span, half_span - 1)
    to_key = np.clip(
        bucket_of(key_side, buckets, distance_cap) + buckets, 0, 2 * buckets - 1
    ).astype(np.int32)
    to_query = np.clip(
        buckets - bucket_of(query_side, buckets, distance_cap), 0, 2 * buckets - 1
    ).astype(np.int32)
    return (to_key, to_query)


def window_tables(query_rows, half_span):
    query_place = np.arange(query_rows)[:, None]
    key_place = np.arange(query_rows + 2 * half_span)[None, :]
    offset = query_place + half_span - key_place
    return (np.abs(offset) < half_span, offset == 0)


def segment_ids(lengths, positions):
    bounds = jnp.cumsum(lengths, axis=-1, dtype=jnp.int32)
    return jnp.sum(
        (bounds[..., None, :] <= positions[:, None]).astype(jnp.int32), axis=-1, dtype=jnp.int32
    )


def product_result(pattern, left_side, right_side):
    return jnp.einsum(pattern, left_side, right_side, preferred_element_type=jnp.float32)


def precise_result(pattern, left_side, right_side):
    return jnp.einsum(pattern, left_side, right_side, precision=PRECISE)


def norm_stats(values):
    centered = values - jnp.mean(values, axis=-1, keepdims=True)
    inverse = lax.rsqrt(jnp.mean(centered * centered, axis=-1, keepdims=True) + EPSILON)
    return (centered * inverse, inverse)


def norm_back(normed, inverse, scale_gain, upstream):
    scaled = upstream * scale_gain
    return inverse * (
        scaled
        - jnp.mean(scaled, axis=-1, keepdims=True)
        - normed * jnp.mean(scaled * normed, axis=-1, keepdims=True)
    )


def adapter_forward(input_rows, weight_matrix, down_low, up_factor_reduced):
    inner_reduced = product_result("sci,sir->scr", input_rows, down_low).astype(jnp.bfloat16)
    mapped_result = product_result(
        "tbr,rv->tbv", input_rows, weight_matrix
    ) + ADAPTER_SCALING * product_result("scr,sro->sco", inner_reduced, up_factor_reduced)
    return (mapped_result, inner_reduced)


def adapter_back(
    input_rows, inner_reduced, weight_matrix, down_low, up_factor_reduced, output_gradient
):
    up_factor_gradient = ADAPTER_SCALING * product_result(
        "myu,myn->mun", inner_reduced, output_gradient
    )
    inner_gradient = (
        ADAPTER_SCALING * product_result("xin,xkn->xik", output_gradient, up_factor_reduced)
    ).astype(jnp.bfloat16)
    grad_down = product_result("sci,scr->sir", input_rows, inner_gradient)
    grad_in = product_result("sco,io->sci", output_gradient, weight_matrix) + product_result(
        "scr,sir->sci", inner_gradient, down_low
    )
    return (grad_in, grad_down, up_factor_gradient)


def skew_rows(values, width):
    head_count, row_count, span = values.shape
    padded = jnp.pad(values, ((0, 0), (0, 0), (0, width + 1 - span)))
    flat = padded.reshape(head_count, row_count * (width + 1))[:, : row_count * width]
    return flat.reshape(head_count, row_count, width)


def query_side_skew(values, width, query_rows):
    return jnp.swapaxes(skew_rows(values, width)[:, :, width - query_rows :], 1, 2)


def score_block(queries, key_block, key_rel, query_rel, allowed):
    score_scale = 1.0 / math.sqrt(3 * queries.shape[2])
    query_rows = queries.shape[0]
    key_rows = key_block.shape[0]
    direct = product_result("qhe,khe->hqk", queries, key_block)
    query_pos = product_result("qhe,nhe->hqn", queries, key_rel)
    key_pos = product_result("khe,phe->hkp", key_block, query_rel)
    raw_score = (
        direct + skew_rows(query_pos, key_rows) + query_side_skew(key_pos, key_rows, query_rows)
    ) * score_scale
    return jnp.where(allowed[None], raw_score, NEGATIVE)


def attention_forward(
    queries, key_block, value_block, pos_query, pos_key, allowed, to_key, to_query
):
    key_rel = jnp.take(pos_key, to_key, axis=0)
    query_rel = jnp.take(pos_query, to_query, axis=0)
    masked = score_block(queries, key_block, key_rel, query_rel, allowed)
    row_top = jnp.max(masked, axis=2, keepdims=True)
    row_exp = jnp.exp(masked - row_top)
    row_total = jnp.sum(row_exp, axis=2, keepdims=True)
    attn_probs = row_exp / row_total
    log_total = (row_top + jnp.log(row_total))[:, :, 0]
    context = product_result("hqk,khe->qhe", attn_probs.astype(jnp.bfloat16), value_block).astype(
        jnp.bfloat16
    )
    return (context, log_total)


def attention_backward(
    queries,
    key_block,
    value_block,
    pos_query,
    pos_key,
    allowed,
    to_key,
    to_query,
    key_hot,
    query_hot,
    log_total,
    grad_context,
):
    score_scale = 1.0 / math.sqrt(3 * queries.shape[2])
    key_rel = jnp.take(pos_key, to_key, axis=0)
    query_rel = jnp.take(pos_query, to_query, axis=0)
    masked = score_block(queries, key_block, key_rel, query_rel, allowed)
    attn_probs = jnp.exp(masked - log_total[:, :, None])
    grad_probs = product_result("qhe,khe->hqk", grad_context, value_block)
    row_delta = jnp.sum(attn_probs * grad_probs, axis=2, keepdims=True)
    grad_score = (attn_probs * (grad_probs - row_delta)).astype(jnp.bfloat16)
    scaled_grad = grad_score.astype(jnp.float32) * score_scale
    head_count, query_rows, key_rows = masked.shape
    span = key_rel.shape[0]

    def key_skew(values):
        return skew_rows(values, key_rows)

    def query_skew(values):
        return query_side_skew(values, key_rows, query_rows)

    grad_query_rel = jax.vjp(key_skew, jnp.zeros((head_count, query_rows, span), jnp.float32))[1](
        scaled_grad
    )[0]
    grad_key_rel = jax.vjp(query_skew, jnp.zeros((head_count, key_rows, span), jnp.float32))[1](
        scaled_grad
    )[0]
    grad_queries = score_scale * product_result(
        "hqk,khe->qhe", grad_score, key_block
    ) + precise_result("hqn,nhe->qhe", grad_query_rel, key_rel.astype(jnp.float32))
    grad_keys = score_scale * product_result("hqk,qhe->khe", grad_score, queries) + precise_result(
        "hkp,phe->khe", grad_key_rel, query_rel.astype(jnp.float32)
    )
    grad_values = product_result("hqk,qhe->khe", attn_probs.astype(jnp.bfloat16), grad_context)
    grad_pos_key = precise_result(
        "nb,nhe->bhe",
        key_hot,
        precise_result("hqn,qhe->nhe", grad_query_rel, queries.astype(jnp.float32)),
    )
    grad_pos_query = precise_result(
        "pb,phe->bhe",
        query_hot,
        precise_result("hkp,khe->phe", grad_key_rel, key_block.astype(jnp.float32)),
    )
    return (grad_queries, grad_keys, grad_values, grad_pos_query, grad_pos_key)


def body(
    tokens,
    cotangent,
    doc_lengths,
    adapter_ids,
    query_weight,
    key_weight,
    value_weight,
    output_weight,
    up_weight,
    down_weight,
    attention_gain,
    feedforward_gain,
    position_gain,
    position_table,
    attention_down,
    attention_up,
    expand_down,
    expand_up,
    reduce_down,
    reduce_up,
):
    narrow_width = jnp.bfloat16
    seq_count = tokens.shape[0]
    model_width = tokens.shape[2]
    head_groups = lax.axis_size("head")
    local_width = model_width // head_groups
    local_heads = HEADS // head_groups
    head_index = lax.axis_index("head")
    block_index = lax.axis_index("seq")
    select = jax.nn.one_hot(adapter_ids, ADAPTERS, dtype=jnp.float32)
    attention_down_factor = precise_result("sa,padr->spdr", select, attention_down).astype(
        narrow_width
    )
    attention_up_factor = precise_result("sa,pard->sprd", select, attention_up).astype(narrow_width)
    exp_down = precise_result("sa,adr->sdr", select, expand_down).astype(narrow_width)
    exp_up = precise_result("sa,arf->srf", select, expand_up).astype(narrow_width)
    red_down = precise_result("sa,afr->sfr", select, reduce_down).astype(narrow_width)
    red_up = precise_result("sa,ard->srd", select, reduce_up).astype(narrow_width)
    token_low = tokens.astype(narrow_width)
    frozen_maps = (query_weight, key_weight, value_weight)
    projected = []
    inners = []
    for member_index in range(3):
        mapped_result, inner_reduced = adapter_forward(
            token_low,
            frozen_maps[member_index],
            attention_down_factor[:, member_index],
            attention_up_factor[:, member_index],
        )
        projected.append(mapped_result.astype(narrow_width))
        inners.append(inner_reduced)
    heads_layout = lax.all_to_all(
        jnp.stack(projected), "head", split_axis=3, concat_axis=2, tiled=True
    )
    query_count = heads_layout.shape[2]
    key_count = query_count + 2 * HALF
    kv_own = heads_layout[1:]
    kv_ext = with_halo(kv_own, (("seq", 2),), HALF)
    to_key_np, to_query_np = relative_tables(HALF, BUCK, SPAN)
    window_np, diagonal_np = window_tables(query_count, HALF)
    to_key = jnp.asarray(to_key_np)
    to_query = jnp.asarray(to_query_np)
    key_hot = jnp.asarray(np.eye(2 * BUCK, dtype=np.float32)[to_key_np])
    query_hot = jnp.asarray(np.eye(2 * BUCK, dtype=np.float32)[to_query_np])
    in_window = jnp.asarray(window_np)
    on_diagonal = jnp.asarray(diagonal_np)
    key_places = block_index * query_count - HALF + jnp.arange(key_count, dtype=jnp.int32)
    key_segments = segment_ids(doc_lengths, key_places)
    inside = (key_places >= 0) & (key_places < query_count * lax.axis_size("seq"))
    key_segments = jnp.where(inside[None, :], key_segments, DOCS)
    query_segments = key_segments[:, HALF : HALF + query_count]
    table_normed, table_inverse = norm_stats(position_table)
    table_reduced = (table_normed * position_gain).astype(narrow_width)

    def shard_columns(matrix):
        return lax.dynamic_slice_in_dim(
            matrix, head_index * local_width, local_width, matrix.ndim - 1
        )

    position_inner_values = []
    pos_tables = []
    for member_index in range(2):
        inner_reduced = product_result(
            "cp,qpa->qca", table_reduced, attention_down_factor[:, member_index]
        ).astype(narrow_width)
        pos_value = product_result(
            "bd,de->be", table_reduced, shard_columns(frozen_maps[member_index])
        )[None] + ADAPTER_SCALING * product_result(
            "cnl,clp->cnp", inner_reduced, shard_columns(attention_up_factor[:, member_index])
        )
        position_inner_values.append(inner_reduced)
        pos_tables.append(pos_value.astype(narrow_width))

    def split_heads(array):
        return array.reshape(array.shape[:-1] + (local_heads, HEAD_DIM))

    queries = split_heads(heads_layout[0])
    pos_query = split_heads(pos_tables[0])
    pos_key = split_heads(pos_tables[1])

    def mask_for(seg_query, seg_key):
        same = (seg_query[:, None] == seg_key[None, :]) & (seg_query[:, None] < DOCS)
        return in_window & same | on_diagonal

    def forward_one(sequence_parts):
        seg_query, seg_key, query_block, key_block, value_block, pos_q_block, pos_k_block = (
            sequence_parts
        )
        return attention_forward(
            query_block,
            key_block,
            value_block,
            pos_q_block,
            pos_k_block,
            mask_for(seg_query, seg_key),
            to_key,
            to_query,
        )

    keys_all = split_heads(kv_ext[0])
    values_all = split_heads(kv_ext[1])
    context, log_total = lax.map(
        forward_one,
        (query_segments, key_segments, queries, keys_all, values_all, pos_query, pos_key),
    )
    context_seq = lax.all_to_all(
        for_sending(context.reshape(seq_count, query_count, local_width)),
        "head",
        split_axis=1,
        concat_axis=2,
        tiled=True,
    )
    attended, inner_out = adapter_forward(
        context_seq, output_weight, attention_down_factor[:, 3], attention_up_factor[:, 3]
    )
    normed_one, inverse_one = norm_stats(tokens + attended)
    hidden = normed_one * attention_gain
    hidden_low = hidden.astype(narrow_width)
    pre_act, inner_up = adapter_forward(hidden_low, up_weight, exp_down, exp_up)
    act_low = jax.nn.gelu(pre_act, approximate=False).astype(narrow_width)
    branch, inner_down = adapter_forward(act_low, down_weight, red_down, red_up)
    normed_two, inverse_two = norm_stats(hidden + branch)
    layer_output = normed_two * feedforward_gain
    grad_two = norm_back(normed_two, inverse_two, feedforward_gain, cotangent)
    grad_act, grad_red_down, grad_red_up = adapter_back(
        act_low, inner_down, down_weight, red_down, red_up, grad_two.astype(narrow_width)
    )
    gelu_pull = jax.vjp(partial(jax.nn.gelu, approximate=False), pre_act)[1]
    grad_act_low = lax.optimization_barrier(grad_act.astype(narrow_width)).astype(jnp.float32)
    grad_pre = gelu_pull(grad_act_low)[0].astype(narrow_width)
    grad_hidden, grad_exp_down, grad_exp_up = adapter_back(
        hidden_low, inner_up, up_weight, exp_down, exp_up, grad_pre
    )
    grad_one = norm_back(normed_one, inverse_one, attention_gain, grad_hidden + grad_two)
    grad_context, grad_out_down, grad_out_up = adapter_back(
        context_seq,
        inner_out,
        output_weight,
        attention_down_factor[:, 3],
        attention_up_factor[:, 3],
        grad_one.astype(narrow_width),
    )
    grad_context_heads = lax.all_to_all(
        grad_context.astype(narrow_width), "head", split_axis=2, concat_axis=1, tiled=True
    )
    kv_back = with_halo(kv_own, (("seq", 2),), HALF)
    keys_back = split_heads(kv_back[0])
    values_back = split_heads(kv_back[1])

    def backward_one(sequence_parts):
        (
            seg_query,
            seg_key,
            query_block,
            key_block,
            value_block,
            pos_q_block,
            pos_k_block,
            total_block,
            grad_block,
        ) = sequence_parts
        return attention_backward(
            query_block,
            key_block,
            value_block,
            pos_q_block,
            pos_k_block,
            mask_for(seg_query, seg_key),
            to_key,
            to_query,
            key_hot,
            query_hot,
            total_block,
            grad_block,
        )

    grad_q, grad_k, grad_v, grad_pos_q, grad_pos_k = lax.map(
        backward_one,
        (
            query_segments,
            key_segments,
            queries,
            keys_back,
            values_back,
            pos_query,
            pos_key,
            log_total,
            split_heads(grad_context_heads),
        ),
    )
    grad_kv = jnp.stack([grad_k, grad_v]).reshape(2, seq_count, key_count, local_width)
    from_above = shifted(grad_kv[:, :, :HALF], "seq", -1)
    from_below = shifted(grad_kv[:, :, HALF + query_count :], "seq", 1)
    own_grad = grad_kv[:, :, HALF : HALF + query_count]
    own_grad = own_grad.at[:, :, query_count - HALF :].add(from_above)
    own_grad = own_grad.at[:, :, :HALF].add(from_below)
    grad_qkv = jnp.concatenate(
        [grad_q.reshape(1, seq_count, query_count, local_width), own_grad]
    ).astype(narrow_width)
    grad_tokens_qkv = lax.all_to_all(grad_qkv, "head", split_axis=2, concat_axis=3, tiled=True)
    input_grad = grad_one
    down_grads = []
    up_grads = []
    for member_index in range(3):
        grad_in, grad_dn, grad_upper = adapter_back(
            token_low,
            inners[member_index],
            frozen_maps[member_index],
            attention_down_factor[:, member_index],
            attention_up_factor[:, member_index],
            grad_tokens_qkv[member_index],
        )
        input_grad = input_grad + grad_in
        down_grads.append(grad_dn)
        up_grads.append(grad_upper)
    down_grads.append(grad_out_down)
    up_grads.append(grad_out_up)
    pos_grads = (
        grad_pos_q.reshape(seq_count, 2 * BUCK, local_width),
        grad_pos_k.reshape(seq_count, 2 * BUCK, local_width),
    )
    table_reduced_widened = table_reduced.astype(jnp.float32)
    grad_table_low = jnp.zeros(position_table.shape, jnp.float32)
    for member_index in range(2):
        position_gradient = pos_grads[member_index]
        weight_cols = shard_columns(frozen_maps[member_index]).astype(jnp.float32)
        up_factor_columns = shard_columns(attention_up_factor[:, member_index]).astype(jnp.float32)
        up_column_gradient = ADAPTER_SCALING * precise_result(
            "ltq,ltu->lqu",
            position_inner_values[member_index].astype(jnp.float32),
            position_gradient,
        )
        position_inner_gradient = ADAPTER_SCALING * precise_result(
            "tda,tka->tdk", position_gradient, up_factor_columns
        )
        grad_table_low = (
            grad_table_low
            + precise_result("sbe,de->bd", position_gradient, weight_cols)
            + precise_result(
                "inm,ilm->nl",
                position_inner_gradient,
                attention_down_factor[:, member_index].astype(jnp.float32),
            )
        )
        down_grads[member_index] = down_grads[member_index] + precise_result(
            "ol,jox->jlx", table_reduced_widened, position_inner_gradient
        )
        placed = lax.dynamic_update_slice_in_dim(
            jnp.zeros_like(up_grads[member_index]), up_column_gradient, head_index * local_width, 2
        )
        up_grads[member_index] = up_grads[member_index] + placed
    table_grad = norm_back(table_normed, table_inverse, position_gain, grad_table_low)
    grad_parts = (
        table_grad,
        precise_result("sa,spdr->padr", select, jnp.stack(down_grads, axis=1)),
        precise_result("sa,sprd->pard", select, jnp.stack(up_grads, axis=1)),
        precise_result("sa,sdr->adr", select, grad_exp_down),
        precise_result("sa,srf->arf", select, grad_exp_up),
        precise_result("sa,sfr->afr", select, grad_red_down),
        precise_result("sa,srd->ard", select, grad_red_up),
    )
    totals = lax.psum(
        (
            grad_parts[0],
            grad_parts[1],
            grad_parts[2],
            grad_parts[3],
            grad_parts[4],
            grad_parts[5],
            grad_parts[6],
        ),
        ("seq", "batch"),
    )
    summed = (
        lax.psum_scatter(totals[0], "head", scatter_dimension=0, tiled=True),
        lax.psum_scatter(totals[1], "head", scatter_dimension=1, tiled=True),
        lax.psum_scatter(totals[2], "head", scatter_dimension=1, tiled=True),
        lax.psum_scatter(totals[3], "head", scatter_dimension=0, tiled=True),
        lax.psum_scatter(totals[4], "head", scatter_dimension=0, tiled=True),
        lax.psum_scatter(totals[5], "head", scatter_dimension=0, tiled=True),
        lax.psum_scatter(totals[6], "head", scatter_dimension=0, tiled=True),
    )
    return (
        layer_output,
        input_grad,
        summed[0],
        summed[1],
        summed[2],
        summed[3],
        summed[4],
        summed[5],
        summed[6],
    )


def solution(mesh):
    return jax.shard_map(
        body,
        mesh=mesh,
        in_specs=(
            P("batch", ("seq", "head"), None),
            P("batch", ("seq", "head"), None),
            P("batch", None),
            P("batch"),
            P(),
            P(),
            P(),
            P(),
            P(),
            P(),
            P(),
            P(),
            P(),
            P(),
            P(),
            P(),
            P(),
            P(),
            P(),
            P(),
        ),
        out_specs=(
            P("batch", ("seq", "head"), None),
            P("batch", ("seq", "head"), None),
            P("head", None),
            P(None, "head", None, None),
            P(None, "head", None, None),
            P("head", None, None),
            P("head", None, None),
            P("head", None, None),
            P("head", None, None),
        ),
        check_vma=False,
    )
```

profile of v0, /device:TPU:0, one launch (start us, length us, event | category | flops | bytes accessed | tf_op | source)
XLA Modules:
  0.0 3683.4 jit_solution(4693099278046917519)
XLA Ops:
  24.1 7.7 copy.181
  31.7 6.1 all-to-all-start
  52.5 7.6 gather_fusion.1
  65.2 7.6 gather_fusion
  82.8 29.0 fusion.44
  134.9 13.2 fusion.180
  148.1 33.3 pad.42.clone
  181.4 106.3 %reshape.1036 = f32[16785408]{0:T(1024)} reshape(f32[8,1024,2049]{2,1,0:T(8,128)} %pad.42.clone) | data formatting | bytes 134283264
  287.7 56.9 %reshape.969 = f32[8,2098176]{1,0:T(8,128)} reshape(f32[16785408]{0:T(1024)} %reshape.1036) | data formatting | bytes 134283264 | tf_op jit(solution)/shard_map/while/body/eval_jaxpr/reshape | solution.py:144
  344.6 44.2 %slice.213 = f32[8,2097152]{1,0:T(8,128)} slice(f32[8,2098176]{1,0:T(8,128)} %reshape.969), slice={[0:8], [0:2097152]} | slice | bytes 134217728 | tf_op jit(solution)/shard_map/while/body/eval_jaxpr/slice | solution.py:144
  401.4 24.9 fusion.181
  426.2 66.4 %pad.43.clone = f32[8,2048,2049]{2,1,0:T(8,128)} pad(f32[8,2048,1024]{2,1,0:T(8,128)} %fusion.181, f32[]{:T(128)} %constant.237.clone.1), padding=0_0x0_0x0_1025 | pad | bytes 201392128 | tf_op jit(solution)/shard_map/while/body/eval_jaxpr/jit(_pad)/pad | solution.py:143
  492.6 212.7 %reshape.1038 = f32[33570816]{0:T(1024)} reshape(f32[8,2048,2049]{2,1,0:T(8,128)} %pad.43.clone) | data formatting | bytes 268566528
  705.3 113.6 %reshape.973 = f32[8,4196352]{1,0:T(8,128)} reshape(f32[33570816]{0:T(1024)} %reshape.1038) | data formatting | bytes 268566528 | tf_op jit(solution)/shard_map/while/body/eval_jaxpr/reshape | solution.py:144
  818.9 86.0 %slice.214 = f32[8,4194304]{1,0:T(8,128)} slice(f32[8,4196352]{1,0:T(8,128)} %reshape.973), slice={[0:8], [0:4194304]} | slice | bytes 268435456 | tf_op jit(solution)/shard_map/while/body/eval_jaxpr/slice | solution.py:144
  904.9 108.8 %copy.266 = f32[1,8,2048,2048]{3,2,1,0:T(8,128)} copy(f32[1,8,2048,2048]{3,1,2,0:T(8,128)} %bitcast.154) | data formatting | bytes 268435456
  1013.7 43.7 %slice.215 = f32[8,2048,1024]{2,1,0:T(8,128)} slice(f32[8,2048,2048]{2,1,0:T(8,128)} %bitcast.449), slice={[0:8], [0:2048], [1024:2048]} | slice | bytes 134217728 | tf_op jit(solution)/shard_map/while/body/eval_jaxpr/slice | solution.py:149
  1057.4 66.8 %copy.228 = f32[8,2048,1024]{1,2,0:T(8,128)} copy(f32[8,2048,1024]{2,1,0:T(8,128)} %slice.215) | data formatting | bytes 134217728
  1124.2 76.7 %fusion.177 = (f32[8,1024]{1,0:T(8,128)S(1)}, f32[8,1024,2048]{2,1,0:T(8,128)}) fusion(f32[8,2048,1024]{1,2,0:T(8,128)} %copy.228, f32[1,8,1024,2048]{3,1,2,0:T(8,128)} %bitcast.152, bf16[1024,8,64]{0,2,1:T(8,128)(2,1)S(1)} %copy-done.12, bf16[2048,8,64]{0,2,1:T(8,128)(2,1)} %bitcast.463, pred[1024,2048]{1,0:T(8,128)(4,1)} %and_or_fusion), kind=kOutput, calls=%fused_computation.313 | convolution fusion | flops 2231361536 | bytes 206602240 | tf_op jit(solution)/shard_map/while/body/eval_jaxpr/qhe,khe->hqk/dot_general | solution.py:95
  1200.9 21.2 fusion.9
  1222.1 24.1 fusion.54
  1250.8 8.0 reduce.13
  1264.7 14.3 copy.219
  1298.0 7.1 fusion.183
  1305.1 21.2 multiply_convert_fusion.1
  1338.3 10.6 fusion.95
  1353.5 8.2 fusion.24
  1363.6 6.9 fusion.37
  1377.3 6.0 copy.196
  1383.3 9.0 reduce.14
  1402.9 10.1 all-to-all-done.2
  1421.8 25.2 fusion.11
  1447.1 44.1 %multiply_reduce_fusion = (f32[8,1024]{1,0:T(8,128)S(1)}, f32[8,1024,2048]{2,1,0:T(8,128)}) fusion(f32[8,1024,2048]{2,1,0:T(8,128)} %get-tuple-element.172, f32[8,1024]{1,0:T(8,128)S(1)} %log_add_fusion, bf16[1024,8,64]{0,2,1:T(8,128)(2,1)S(1)} %squeeze.82, bf16[2048,8,64]{0,2,1:T(8,128)(2,1)S(1)} %bitcast.487), kind=kOutput, calls=%fused_computation.12 | convolution fusion | flops 2197807104 | bytes 137428992 | tf_op jit(solution)/shard_map/while/body/eval_jaxpr/qhe,khe->hqk/dot_general | solution.py:95
  1491.2 10.9 copy.202
  1502.0 75.3 %fusion.4 = (f32[1,8,1024,2048]{3,2,1,0:T(8,128)}, bf16[8,1024,2048]{2,1,0:T(8,128)(2,1)}) fusion(f32[8,1024,2048]{2,1,0:T(8,128)} %get-tuple-element.180, f32[8,1024]{1,0:T(8,128)S(1)} %get-tuple-element.179, f32[8,1024,2048]{2,1,0:T(8,128)} %get-tuple-element.172, f32[8,1024]{1,0:T(8,128)S(1)} %log_add_fusion), kind=kLoop, calls=%fused_computation.10 | loop fusion | flops 100663296 | bytes 234946560
  1577.3 56.5 %copy.234 = f32[1,8,1024,2048]{3,1,2,0:T(8,128)} copy(f32[1,8,1024,2048]{3,2,1,0:T(8,128)} %get-tuple-element.154) | data formatting | bytes 134217728
  1633.8 44.2 %pad.44 = f32[8,2098176]{1,0:T(8,128)} pad(f32[8,2097152]{1,0:T(8,128)} %bitcast.158, f32[]{:T(128)} %constant.237.clone.1), padding=0_0x0_1024 | pad | bytes 134250496 | tf_op jit(solution)/shard_map/while/body/eval_jaxpr/transpose(jvp())/pad | solution.py:144
  1678.1 211.5 %reshape.1042 = f32[16785408]{0:T(1024)} reshape(f32[8,2098176]{1,0:T(8,128)} %pad.44) | data formatting | bytes 134283264
  1889.5 103.7 %reshape.984 = f32[8,1024,2049]{2,1,0:T(8,128)} reshape(f32[16785408]{0:T(1024)} %reshape.1042) | data formatting | bytes 134283264 | tf_op jit(solution)/shard_map/while/body/eval_jaxpr/transpose(jvp())/reshape | solution.py:144
  1993.2 22.4 fusion.17
  2015.6 32.3 fusion.3
  2047.9 70.3 %copy.231 = f32[8,2048,1024]{2,1,0:T(8,128)} copy(f32[8,2048,1024]{1,2,0:T(8,128)} %fusion.3) | data formatting | bytes 134217728
  2118.2 65.1 %pad_bitcast_fusion = f32[1,8,2048,2048]{3,2,1,0:T(8,128)} fusion(f32[8,2048,1024]{2,1,0:T(8,128)} %copy.231), kind=kLoop, calls=%fused_computation.3 | loop fusion | bytes 201326592
  2183.3 108.8 %copy.235 = f32[1,8,2048,2048]{3,1,2,0:T(8,128)} copy(f32[1,8,2048,2048]{3,2,1,0:T(8,128)} %pad_bitcast_fusion) | data formatting | bytes 268435456
  2292.1 88.8 %pad.47 = f32[8,4196352]{1,0:T(8,128)} pad(f32[8,4194304]{1,0:T(8,128)} %bitcast.160, f32[]{:T(128)} %constant.237.clone.1), padding=0_0x0_2048 | pad | bytes 268500992 | tf_op jit(solution)/shard_map/while/body/eval_jaxpr/transpose(jvp())/pad | solution.py:144
  2381.0 425.3 %reshape.1040 = f32[33570816]{0:T(1024)} reshape(f32[8,4196352]{1,0:T(8,128)} %pad.47) | data formatting | bytes 268566528
  2806.3 207.2 %reshape.986 = f32[8,2048,2049]{2,1,0:T(8,128)} reshape(f32[33570816]{0:T(1024)} %reshape.1040) | data formatting | bytes 268566528 | tf_op jit(solution)/shard_map/while/body/eval_jaxpr/transpose(jvp())/reshape | solution.py:144
  3013.6 39.9 %fusion.7 = f32[8,64,2048]{2,1,0:T(8,128)} fusion(bf16[1024,8,64]{0,2,1:T(8,128)(2,1)} %copy.191, f32[8,2048,2049]{2,1,0:T(8,128)} %reshape.986), kind=kOutput, calls=%fused_computation.18 | convolution fusion | flops 12884901888 | bytes 72351744 | tf_op jit(solution)/shard_map/while/body/eval_jaxpr/hkp,phe->khe/dot_general | solution.py:99
  3053.5 19.7 multiply_add_fusion.1
  3073.2 10.9 copy.201
  3089.4 18.3 add_convert_fusion.1
  3113.7 6.2 fusion.33
  3119.9 16.9 collective-permute-done.2
  3136.8 6.5 pad_maximum_fusion.3
  3151.1 37.0 %fusion.5 = f32[8,64,1024]{2,1,0:T(8,128)} fusion(bf16[2048,8,64]{0,2,1:T(8,128)(2,1)} %bitcast.465, f32[8,2048,2049]{2,1,0:T(8,128)} %reshape.986), kind=kOutput, calls=%fused_computation.16 | convolution fusion | flops 12884901888 | bytes 71303168 | tf_op jit(solution)/shard_map/while/body/eval_jaxpr/hkp,khe->phe/dot_general | solution.py:99
  3211.9 18.5 fusion.15
  3241.8 14.4 all-to-all-done.3
  3313.5 78.9 %all-reduce.14.cloned.1.call-done = (f32[4,8,1024,16]{2,3,1,0:T(8,128)}, f32[4,8,16,1024]{3,2,1,0:T(8,128)}) async-done(((f32[4,8,1024,16]{2,3,1,0:T(8,128)}, f32[4,8,16,1024]{3,2,1,0:T(8,128)}), (f32[4,8,1024,16]{2,3,1,0:T(8,128)}, f32[4,8,16,1024]{3,2,1,0:T(8,128)})) %all-reduce.14.cloned.1.call-update) | async-done | bytes 4194320
  3396.0 13.4 reduce-scatter.20.cloned.1.call-done
  3409.4 16.8 reduce-scatter.14.cloned.1.call-done
  3426.2 34.0 reduce-scatter.18.cloned.1.call-done
  3460.2 34.0 reduce-scatter.16.cloned.1.call-done
  3494.2 34.6 reduce-scatter.12.cloned.1.call-done
  3537.7 130.9 %all-reduce.12.cloned.1.call-done = (f32[256,1024]{1,0:T(8,128)}, f32[4,4,1024,16]{2,3,1,0:T(8,128)}, f32[4,4,16,1024]{3,2,1,0:T(8,128)}, f32[4,1024,16]{1,2,0:T...) async-done(((f32[256,1024]{1,0:T(8,128)}, f32[4,4,1024,16]{2,3,1,0:T(8,128)}, f32[4,4,16,1024]{3,2,1,0:T(8,128)}, ...) | async-done | bytes 5767184 | tf_op jit(solution)/shard_map/psum | solution.py:522
  (398 shorter events, 285.9 us)
Async XLA Ops:
  7.2 12.2 copy-start
  7.2 4.8 copy-start.31
  12.0 30.9 copy-start.36
  12.2 7.2 copy-start.5
  12.6 9.0 copy-start.69
  13.0 7.7 copy-start.65
  13.3 7.8 copy-start.67
  16.4 21.4 copy-start.41
  31.7 80.0 %all-to-all-start = ((bf16[3,1,512,1024]{2,0,1,3:T(4,128)(2,1)}), bf16[3,1,512,1024]{2,0,1,3:T(4,128)(2,1)}, u32[]{:S(2)}, u32[]{:S(2)}) async-start(bf16[3,1,512,1024]{2,0,1,3:T(4,128)(2,1)} %copy.181), calls=%async_computation | async-start | bytes 8388608 | tf_op jit(solution)/shard_map/all_to_all | solution.py:292
  37.9 9.3 copy-start.83
  37.9 11.6 copy-start.85
  37.9 3.9 copy-start.95
  42.9 4.3 copy-start.73
  43.2 6.3 copy-start.71
  77.4 5.4 copy-start.35
  124.3 10.6 copy-start.11
  124.3 10.6 copy-start.21
  127.7 261.1 %collective-permute-start = (bf16[2,1,512,512]{3,2,0,1:T(8,128)(2,1)}, bf16[2,1,512,512]{3,2,0,1:T(8,128)(2,1)}, u32[]{:S(2)}, u32[]{:S(2)}) collective-permute-start(bf16[2,1,512,512]{3,2,0,1:T(8,128)(2,1)} %get-tuple-element.167), channel_id=1, source_target_pairs={{0,4},{4,8},{8,12},{12,16},{16,20},{20,24},{24,28},{1,5},{5,9},{9,... | collective-permute-start | bytes 3145736 | tf_op jit(solution)/shard_map/ppermute | solution.py:33
  133.6 255.2 %collective-permute-start.1 = (bf16[2,1,512,512]{3,2,0,1:T(8,128)(2,1)}, bf16[2,1,512,512]{3,2,0,1:T(8,128)(2,1)}, u32[]{:S(2)}, u32[]{:S(2)}) collective-permute-start(bf16[2,1,512,512]{3,2,0,1:T(8,128)(2,1)} %get-tuple-element.168), channel_id=1, source_target_pairs={{4,0},{8,4},{12,8},{16,12},{20,16},{24,20},{28,24},{5,1},{9,5},{13... | collective-permute-start | bytes 3145736 | tf_op jit(solution)/shard_map/ppermute | solution.py:35
  397.4 4.0 copy-start.23
  1057.4 66.8 %copy-start.12 = (bf16[1024,8,64]{0,2,1:T(8,128)(2,1)S(1)}, bf16[1024,8,64]{0,2,1:T(8,128)(2,1)}, u32[]{:S(2)}) copy-start(bf16[1024,8,64]{0,2,1:T(8,128)(2,1)} %copy-done.11) | copy-start | bytes 3145732
  1200.9 21.2 copy-start.57
  1222.1 24.1 copy-start.81
  1258.8 5.8 copy-start.64
  1260.4 25.5 all-to-all-start.1
  1287.7 4.4 copy-start.37
  1298.0 7.1 copy-start.87
  1298.0 7.1 copy-start.50
  1298.0 30.3 slice-start
  1305.0 21.3 copy-start.44
  1305.1 23.2 slice-start.1
  1328.3 4.5 copy-start.77
  1328.3 4.5 copy-start.59
  1337.9 32.7 copy-start.8
  1338.3 10.6 copy-start.75
  1363.6 7.0 copy-start.79
  1392.3 7.1 copy-start.58
  1392.3 7.1 copy-start.82
  1394.9 18.1 all-to-all-start.2
  1421.8 25.3 copy-start.29
  1889.5 103.7 %copy-start.22 = (bf16[1024,8,64]{0,2,1:T(8,128)(2,1)S(1)}, bf16[1024,8,64]{0,2,1:T(8,128)(2,1)}, u32[]{:S(2)}) copy-start(bf16[1024,8,64]{0,2,1:T(8,128)(2,1)} %copy.188) | copy-start | bytes 3145732
  3013.6 39.9 %copy-start.13 = (bf16[1024,8,64]{0,2,1:T(8,128)(2,1)S(1)}, bf16[1024,8,64]{0,2,1:T(8,128)(2,1)}, u32[]{:S(2)}) copy-start(bf16[1024,8,64]{0,2,1:T(8,128)(2,1)} %copy-done.11) | copy-start | bytes 3145732
  3088.1 48.7 %collective-permute-start.2 = (f32[2,1,512,512]{3,0,1,2:T(2,128)}, f32[2,1,512,512]{3,0,1,2:T(2,128)}, u32[]{:S(2)}, u32[]{:S(2)}) collective-permute-start(f32[2,1,512,512]{3,0,1,2:T(2,128)} %fusion.39), channel_id=1, source_target_pairs={{4,0},{8,4},{12,8},{16,12},{20,16},{24,20},{28,24},{5,1},{9,5},{13... | collective-permute-start | bytes 6291464 | tf_op jit(solution)/shard_map/ppermute | solution.py:53
  3113.7 23.1 copy-start.1
  3113.7 23.1 copy-start.2
  3145.3 47.3 %collective-permute-start.3 = (f32[2,1,512,512]{3,0,1,2:T(2,128)}, f32[2,1,512,512]{3,0,1,2:T(2,128)}, u32[]{:S(2)}, u32[]{:S(2)}) collective-permute-start(f32[2,1,512,512]{3,0,1,2:T(2,128)} %get-tuple-element.158), channel_id=1, source_target_pairs={{0,4},{4,8},{8,12},{12,16},{16,20},{20,24},{24,28},{1,5},{5,9},{9,... | collective-permute-start | bytes 6291464 | tf_op jit(solution)/shard_map/ppermute | solution.py:53
  3197.1 3.8 copy-start.34
  3206.3 49.9 %all-to-all-start.3 = ((bf16[3,1,1024,512]{3,0,1,2:T(4,128)(2,1)}), bf16[3,1,1024,512]{3,0,1,2:T(4,128)(2,1)}, u32[]{:S(2)}, u32[]{:S(2)}) async-start(bf16[3,1,1024,512]{3,0,1,2:T(4,128)(2,1)} %pad_maximum_fusion.1), calls=%async_computation.3 | async-start | bytes 8388608 | tf_op jit(solution)/shard_map/all_to_all | solution.py:460
  3211.9 180.6 %all-reduce.14.cloned.1.call-start = ((), (), s32[]{:S(2)}) async-start(), calls=%async_computation.15 | async-start | bytes 8388608
  3230.4 5.9 copy-start.86
  3230.4 6.4 copy-start.24
  3230.4 6.4 copy-start.33
  3236.8 4.6 copy-start.84
  3260.9 3.9 copy-start.70
  3264.8 5.4 copy-start.68
  3270.2 5.5 copy-start.66
  3271.8 5.6 copy-start.74
  3274.1 3.9 copy-start.6
  3283.9 125.5 %reduce-scatter.20.cloned.1.call-start = ((), (), s32[]{:S(2)}) async-start(), calls=%async_computation.13 | async-start | bytes 786432 | tf_op jit(solution)/shard_map/reduce_scatter | solution.py:541
  3287.3 138.9 %reduce-scatter.14.cloned.1.call-start = ((), (), s32[]{:S(2)}) async-start(), calls=%async_computation.10 | async-start | bytes 786432 | tf_op jit(solution)/shard_map/reduce_scatter | solution.py:538
  3289.8 170.4 %reduce-scatter.18.cloned.1.call-start = ((), (), s32[]{:S(2)}) async-start(), calls=%async_computation.12 | async-start | bytes 3145728 | tf_op jit(solution)/shard_map/reduce_scatter | solution.py:540
  3294.5 199.7 %reduce-scatter.16.cloned.1.call-start = ((), (), s32[]{:S(2)}) async-start(), calls=%async_computation.11 | async-start | bytes 3145728 | tf_op jit(solution)/shard_map/reduce_scatter | solution.py:539
  3299.0 229.8 %reduce-scatter.12.cloned.1.call-start = ((), (), s32[]{:S(2)}) async-start(), calls=%async_computation.9 | async-start | bytes 3145728 | tf_op jit(solution)/shard_map/reduce_scatter | solution.py:535
  3311.7 356.8 %all-reduce.12.cloned.1.call-start = ((), (), s32[]{:S(2)}) async-start(), calls=%async_computation.14 | async-start | bytes 11534336 | tf_op jit(solution)/shard_map/psum | solution.py:522
  (56 other events, 122.7 us)
Sparse Core Ops, SparseCore 0:
  3284.0 108.4 all-reduce.13
  3394.8 14.5 reduce-scatter.19
  3411.6 14.5 reduce-scatter.13
  3428.4 31.8 reduce-scatter.17
  3462.3 31.8 reduce-scatter.15
  3497.0 31.8 reduce-scatter.11
  3534.0 134.4 all-reduce.11
where the time goes:
time: 3700 us; the launch traced here: 3680 us
  local copies, waits for them, and re-layouts  2490 us (67%)
  matrix products  540 us (15%)
  waiting for transfers between devices  389 us (11%)
  other arithmetic  214 us (6%)
    unnamed x239, local copies, waits for them, and re-layouts  1470 us
    reshape x4, local copies, waits for them, and re-layouts, skew_rows(): padded.reshape(head_count, row_count * (width + 1))[:, :row_count * width]  481 us
    dot_general x60, matrix products, product_result(): jnp.einsum(pattern, left_side, right_side, preferred_element_type=jnp.flo...  319 us
    dot_general x20, matrix products, precise_result(): return jnp.einsum(pattern, left_side, right_side, precision=PRECISE)  174 us
    pad x2, local copies, waits for them, and re-layouts, skew_rows(): padded.reshape(head_count, row_count * (width + 1))[:, :row_count * width]  133 us
    psum x1, waiting for transfers between devices, body(): lax.psum((grad_parts[0], grad_parts[1], grad_parts[2], grad_parts[3], gra...  131 us
    slice x2, local copies, waits for them, and re-layouts, skew_rows(): padded.reshape(head_count, row_count * (width + 1))[:, :row_count * width]  130 us
    pad x2, local copies, waits for them, and re-layouts, skew_rows(): padded = jnp.pad(values, ((0, 0), (0, 0), (0, width + 1 - span)))  99.7 us
  transfers between devices with their start and end apart: 15, of which 11 were waited for; matrix products, arithmetic and copies ran while one was open for 13% of the time, Pallas kernels for 0%

commit v1 on v0

v1 whole, which is shorter than its diff:
```python
from functools import partial
import math

import jax
import jax.numpy as jnp
import numpy as np
from jax import lax
from jax.experimental import pallas as pl
from jax.experimental.pallas import tpu as pltpu
from jax.sharding import PartitionSpec as P

HEADS = 16
HEAD_DIM = 64
BUCK = 256
SPAN = 512
ADAPTERS = 8
HALF = 512
DOCS = 8

EPSILON = 1e-07
ADAPTER_SCALING = 2.0
NEGATIVE = -1e30
PRECISE = lax.Precision.HIGHEST
TILE = 128
BF = jnp.bfloat16
F32 = jnp.float32
NN = (((1,), (0,)), ((), ()))
NT = (((1,), (1,)), ((), ()))


def mm(a, b, dims=NN):
    return lax.dot_general(a, b, dims, preferred_element_type=F32)

def lanes(shape=(TILE, TILE)):
    return lax.broadcasted_iota(jnp.int32, shape, 1)

def rows(shape=(TILE, TILE)):
    return lax.broadcasted_iota(jnp.int32, shape, 0)

def skew(tile):
    return pltpu.roll(tile, 0, 1, stride=1, stride_axis=0)

def flip_matrix():
    return jnp.where(lanes() + rows() == TILE - 1, 1.0, 0.0).astype(BF)


def forward_kernel(q_ref, k_ref, v_ref, pk_ref, pq_ref, qhot_ref, kbias_ref,
                   ctx_ref, p_ref, ctxf_ref, inv_ref,
                   qs_ref, kz_ref, vz_ref, ks_ref, s_ref):
    rows_q = q_ref.shape[1]
    tiles = rows_q // TILE
    span = 2 * HALF // TILE
    width = (span + 1) * TILE
    flip = flip_matrix()
    factor = math.log2(math.e) / math.sqrt(3 * HEAD_DIM)
    k = k_ref[0]
    v = v_ref[0]
    kb = kbias_ref[0]
    kcol = lanes(k.shape) < HEAD_DIM
    below = lanes() + rows() < TILE
    place = lanes() + rows()
    qcol = lanes((rows_q, TILE)) < HEAD_DIM
    tcol = lanes() < HEAD_DIM
    for h in range(2):
        own = kcol if h == 0 else ~kcol
        kz_ref[h] = jnp.where(own, k, kb)
        vz_ref[h] = jnp.where(own, v, jnp.ones_like(v))
        km = jnp.where(own, k, jnp.zeros_like(k))
        for d in range(span + 1):
            lo = max(span - 1 - d, 0) * TILE
            hi = min(span + 1 - d, span) * TILE
            key_rel = mm(km[d * TILE:d * TILE + rows_q], pq_ref[0, lo:hi, :], NT).astype(BF)
            for t in range(tiles):
                part = key_rel[t * TILE:(t + 1) * TILE]
                if d == 0 or d == span:
                    picked = part
                else:
                    picked = jnp.where(below, part[:, TILE:], part[:, :TILE])
                ks_ref[h, t, d * TILE:(d + 1) * TILE, :] = skew(picked)
        q_masked = jnp.where(qcol if h == 0 else ~qcol, q_ref[0], jnp.zeros_like(q_ref[0]))
        query_rel = mm(q_masked, pk_ref[0], NT).astype(BF)
        for t in range(tiles):
            part = query_rel[t * TILE:(t + 1) * TILE]
            for d in range(span + 1):
                if d == 0:
                    picked = part[:, :TILE]
                elif d == span:
                    picked = part[:, (span - 1) * TILE:]
                else:
                    picked = jnp.where(below, part[:, d * TILE:(d + 1) * TILE], part[:, (d - 1) * TILE:d * TILE])
                qs_ref[h, t, :, d * TILE:(d + 1) * TILE] = skew(picked)

    def tile_step(t, carry):
        base = pl.multiple_of(t * TILE, TILE)
        q = q_ref[0, pl.ds(base, TILE), :]
        hot = qhot_ref[0, pl.ds(base, TILE), :]
        a = t % 2
        outs = []
        for h in range(2):
            own = tcol if h == 0 else ~tcol
            q_side = mm(flip, jnp.where(own, q, hot)).astype(BF)
            left = jnp.concatenate([q_side, flip], axis=1)
            right = jnp.concatenate([kz_ref[h, pl.ds(base, width), :], ks_ref[h, t]], axis=1)
            s_ref[h] = mm(left, right, NT) + mm(flip, qs_ref[h, t])
        for h in range(2):
            own = tcol if h == 0 else ~tcol
            first = s_ref[h, :, :TILE]
            s_ref[h, :, :TILE] = jnp.where(place > TILE - 1, first, NEGATIVE)
            last = s_ref[h, :, span * TILE:]
            s_ref[h, :, span * TILE:] = jnp.where(place < TILE - 1, last, NEGATIVE)
            mid = s_ref[h, :, (span // 2) * TILE:(span // 2 + 1) * TILE]
            s_ref[h, :, (span // 2) * TILE:(span // 2 + 1) * TILE] = jnp.where((place == TILE - 1) & (mid < 0.1 * NEGATIVE), 0.0, mid)
            top = s_ref[h, :, :TILE]
            for d in range(1, span + 1):
                top = jnp.maximum(top, s_ref[h, :, d * TILE:(d + 1) * TILE])
            peak = jnp.max(top, axis=1, keepdims=True)
            prob = jnp.exp2((s_ref[h] - peak) * factor).astype(BF)
            p_ref[0, h, t // 2, pl.ds(pl.multiple_of(a * TILE, TILE), TILE), pl.ds(pl.multiple_of(a * TILE, TILE), width)] = prob
            total = mm(prob, vz_ref[h, pl.ds(base, width), :])
            swapped = pltpu.roll(total, HEAD_DIM, 1)
            den = jnp.where(own, swapped, total)
            inv = 1.0 / den
            inv_ref[0, h, pl.ds(base, TILE), :] = inv
            p_ref[0, h, t // 2, pl.ds(pl.multiple_of(a * TILE, TILE), TILE), pl.ds(pl.multiple_of((1 - a) * width, TILE), TILE)] = jnp.zeros((TILE, TILE), BF)
            outs.append(total * inv)
        ctx = jnp.where(tcol, outs[0], outs[1])
        ctxf_ref[0, pl.ds(base, TILE), :] = ctx
        ctx_ref[0, pl.ds(base, TILE), :] = mm(flip, ctx.astype(BF)).astype(BF)
        return carry

    lax.fori_loop(0, tiles, tile_step, 0, unroll=True)


def attention_forward(q, kext, vext, pk, pq, qhot, kbias):
    n, rq, width = q.shape
    rk = kext.shape[1]
    pairs = width // TILE
    off = 2 * HALF
    def col(r):
        return pl.BlockSpec((1, r, TILE), lambda s, p: (s, 0, p))
    def whole(r):
        return pl.BlockSpec((1, r, TILE), lambda s, p: (s, 0, 0))
    wide = off + 2 * TILE
    return pl.pallas_call(
        forward_kernel,
        grid=(n, pairs),
        in_specs=[col(rq), col(rk), col(rk), col(off), col(off), whole(rq), whole(rk)],
        out_specs=[col(rq),
                   pl.BlockSpec((1, 2, rq // (2 * TILE), 2 * TILE, wide), lambda s, p: (s, p, 0, 0, 0)),
                   col(rq),
                   pl.BlockSpec((1, 2, rq, TILE), lambda s, p: (s, p, 0, 0))],
        out_shape=[jax.ShapeDtypeStruct((n, rq, width), BF),
                   jax.ShapeDtypeStruct((n, 2 * pairs, rq // (2 * TILE), 2 * TILE, wide), BF),
                   jax.ShapeDtypeStruct((n, rq, width), F32),
                   jax.ShapeDtypeStruct((n, 2 * pairs, rq, TILE), F32)],
        scratch_shapes=[pltpu.VMEM((2, rq // TILE, TILE, off + TILE), BF),
                        pltpu.VMEM((2, rk, TILE), BF), pltpu.VMEM((2, rk, TILE), BF),
                        pltpu.VMEM((2, rq // TILE, off + TILE, TILE), BF),
                        pltpu.VMEM((2, TILE, off + TILE), F32)],
        compiler_params=pltpu.CompilerParams(dimension_semantics=("arbitrary", "arbitrary"), vmem_limit_bytes=48 * 2**20),
        name="attention_forward",
    )(q, kext, vext, pk, pq, qhot, kbias)


def backward_kernel(q_ref, k_ref, v_ref, pk_ref, pq_ref, p_ref, g_ref, ctxf_ref, inv_ref,
                    dq_ref, dk_ref, dv_ref, dpk_ref, dpq_ref,
                    qr_ref, gr_ref, e_ref, gc_ref, gk_ref, dvt_ref):
    rows_q = q_ref.shape[1]
    rows_k = k_ref.shape[1]
    tiles = rows_q // TILE
    key_tiles = rows_k // TILE
    span = 2 * HALF // TILE
    wide = (span + 2) * TILE
    flip = flip_matrix()
    scale = 1.0 / math.sqrt(3 * HEAD_DIM)
    tcol = lanes() < HEAD_DIM
    qcol = lanes((rows_q, TILE)) < HEAD_DIM
    over = lanes() > rows()
    under = lanes() >= rows()

    @pl.when((pl.program_id(0) == 0) & (pl.program_id(1) == 0))
    def _():
        gk_ref[...] = jnp.zeros_like(gk_ref)

    for t in range(tiles):
        at = slice(t * TILE, (t + 1) * TILE)
        qr_ref[at] = mm(flip, q_ref[0, at]).astype(BF)
        gr_ref[at] = mm(flip, g_ref[0, at]).astype(BF)
    q_rev = qr_ref[...]
    g_rev = gr_ref[...]
    q_turned = q_rev.T
    k_turned = k_ref[0].T
    product = g_rev.astype(F32) * ctxf_ref[0]
    dvt_ref[...] = jnp.zeros_like(dvt_ref)
    dq_parts = []
    dk_parts = []
    for h in range(2):
        own = qcol if h == 0 else ~qcol
        part = slice(h * HEAD_DIM, (h + 1) * HEAD_DIM)
        g_masked = jnp.where(own, g_rev, jnp.zeros_like(g_rev))
        inv = inv_ref[0, h]
        delta = jnp.sum(jnp.where(own, product, 0.0), axis=1, keepdims=True) * inv
        g_turned = (g_rev.astype(F32) * inv).astype(BF).T[part]
        dq_main = []
        for u in range(tiles // 2):
            at = slice(u * 2 * TILE, (u + 1) * 2 * TILE)
            window = slice(u * 2 * TILE, u * 2 * TILE + wide)
            prob = p_ref[0, h, u]
            g_probs = mm(g_masked[at], v_ref[0, window], NT)
            inv_u = jnp.concatenate([inv[at]] * (span + 2), axis=1)
            delta_u = jnp.concatenate([delta[at]] * (span + 2), axis=1)
            e = (prob.astype(F32) * (g_probs * inv_u - delta_u)).astype(BF)
            e_ref[h, u] = e
            dvt_ref[part, window] += mm(g_turned[:, at], prob)
            dq_main.append(mm(e, k_ref[0, window]))
            for a in range(2):
                for t in range(span):
                    def turned(d):
                        return pltpu.roll(e_ref[h, u, a * TILE:(a + 1) * TILE, (a + d) * TILE:(a + d + 1) * TILE], 1, 1, stride=1, stride_axis=0)
                    here = turned(t) if t == 0 else after
                    after = turned(t + 1)
                    gc_ref[h, (2 * u + a) * TILE:(2 * u + a + 1) * TILE, t * TILE:(t + 1) * TILE] = jnp.where(over, after, here)
        dq_parts.append(jnp.concatenate(dq_main, axis=0) + mm(gc_ref[h], pk_ref[0]))
        dpk_ref[0, part, :] = mm(q_turned[part], gc_ref[h]) * scale
        dk_tiles = []
        for kt in range(key_tiles):
            dlow = max(0, kt - tiles + 1)
            dhigh = min(span, kt)
            flat = []
            spun = {}
            for d in range(dlow, dhigh + 1):
                qt = kt - d
                a = qt % 2
                et = e_ref[h, qt // 2, a * TILE:(a + 1) * TILE, (a + d) * TILE:(a + d + 1) * TILE].T
                flat.append((qt, et))
                spun[d] = skew(et)
            tlow = max(dlow - 1, 0)
            thigh = min(dhigh, span - 1)
            for t in range(tlow, thigh + 1):
                zero = jnp.zeros((TILE, TILE), BF)
                gk_ref[h, kt * TILE:(kt + 1) * TILE, t * TILE:(t + 1) * TILE] = jnp.where(under, spun.get(t + 1, zero), spun.get(t, zero))
            flat = flat[::-1]
            left = jnp.concatenate([et for _, et in flat] + [gk_ref[h, kt * TILE:(kt + 1) * TILE, tlow * TILE:(thigh + 1) * TILE]], axis=1)
            right = jnp.concatenate([q_rev[flat[0][0] * TILE:(flat[-1][0] + 1) * TILE], pq_ref[0, tlow * TILE:(thigh + 1) * TILE]], axis=0)
            dk_tiles.append(mm(left, right))
        dk_parts.append(jnp.concatenate(dk_tiles, axis=0))
        dpq_ref[0, part, :] = mm(k_turned[part], gk_ref[h]) * scale
    dq = (jnp.where(qcol, dq_parts[0], dq_parts[1]) * scale).astype(BF)
    for t in range(tiles):
        at = slice(t * TILE, (t + 1) * TILE)
        dq_ref[0, at] = mm(flip, dq[at]).astype(BF)
    kcol = lanes((rows_k, TILE)) < HEAD_DIM
    dk_ref[0] = (jnp.where(kcol, dk_parts[0], dk_parts[1]) * scale).astype(BF)
    dv_ref[0] = dvt_ref[...].astype(BF).T


def attention_backward(q, kext, vext, pk, pq, probs, g, ctxf, inv):
    n, rq, width = q.shape
    rk = kext.shape[1]
    pairs = width // TILE
    off = 2 * HALF
    wide = off + 2 * TILE
    def col(r):
        return pl.BlockSpec((1, r, TILE), lambda s, p: (s, 0, p))
    def row(r):
        return pl.BlockSpec((1, TILE, r), lambda s, p: (s, p, 0))
    return pl.pallas_call(
        backward_kernel,
        grid=(n, pairs),
        in_specs=[col(rq), col(rk), col(rk), col(off), col(off),
                  pl.BlockSpec((1, 2, rq // (2 * TILE), 2 * TILE, wide), lambda s, p: (s, p, 0, 0, 0)),
                  col(rq), col(rq),
                  pl.BlockSpec((1, 2, rq, TILE), lambda s, p: (s, p, 0, 0))],
        out_specs=[col(rq), col(rk), col(rk), row(off), row(off)],
        out_shape=[jax.ShapeDtypeStruct((n, rq, width), BF),
                   jax.ShapeDtypeStruct((n, rk, width), BF),
                   jax.ShapeDtypeStruct((n, rk, width), BF),
                   jax.ShapeDtypeStruct((n, width, off), F32),
                   jax.ShapeDtypeStruct((n, width, off), F32)],
        scratch_shapes=[pltpu.VMEM((rq, TILE), BF), pltpu.VMEM((rq, TILE), BF),
                        pltpu.VMEM((2, rq // (2 * TILE), 2 * TILE, wide), BF),
                        pltpu.VMEM((2, rq, off), BF),
                        pltpu.VMEM((2, rk, off), BF),
                        pltpu.VMEM((TILE, rk), F32)],
        compiler_params=pltpu.CompilerParams(dimension_semantics=("arbitrary", "arbitrary"), vmem_limit_bytes=56 * 2**20),
        name="attention_backward",
    )(q, kext, vext, pk, pq, probs, g, ctxf, inv)


def shifted(value, axes, steps):
    count = math.prod(lax.axis_size(axis) for axis in axes)
    initial, last = (max(0, -steps), min(count, count - steps))
    return lax.ppermute(value, axes, [(source, source + steps) for source in range(initial, last)])


def bucket_of(offset, buckets, distance_cap):
    middle = buckets // 2
    sign_of = np.sign(offset)
    magnitude = np.where((offset < middle) & (offset > -middle), middle - 1, np.abs(offset))
    log_place = (
        np.ceil(np.log(magnitude / middle) / np.log((distance_cap - 1) / middle) * (middle - 1))
        + middle
    )
    return np.where(np.abs(offset) <= middle, offset, log_place * sign_of).astype(np.int32)


def offset_tables():
    place = np.arange(2 * HALF)

    def hot(distance, sign):
        clipped = np.clip(distance, 1 - HALF, HALF - 1)
        bucket = np.clip(BUCK + sign * bucket_of(clipped, BUCK, SPAN), 0, 2 * BUCK - 1)
        return np.eye(2 * BUCK, dtype=np.float32)[bucket]

    return hot(HALF - place, 1), hot(place - HALF, -1), hot(HALF - 1 - place, -1)


def segment_ids(lengths, positions):
    bounds = jnp.cumsum(lengths, axis=-1, dtype=jnp.int32)
    return jnp.sum(
        (bounds[..., None, :] <= positions[:, None]).astype(jnp.int32), axis=-1, dtype=jnp.int32
    )


def product(pattern, left_side, right_side):
    return jnp.einsum(pattern, left_side, right_side, preferred_element_type=F32)


def split_product(pattern, exact, wide):
    high = wide.astype(BF)
    low = (wide - high.astype(F32)).astype(BF)
    return product(pattern, exact, high) + product(pattern, exact, low)


def norm_stats(values):
    centered = values - jnp.mean(values, axis=-1, keepdims=True)
    inverse = lax.rsqrt(jnp.mean(centered * centered, axis=-1, keepdims=True) + EPSILON)
    return (centered * inverse, inverse)


def norm_back(normed, inverse, scale_gain, upstream):
    scaled = upstream * scale_gain
    return inverse * (
        scaled
        - jnp.mean(scaled, axis=-1, keepdims=True)
        - normed * jnp.mean(scaled * normed, axis=-1, keepdims=True)
    )


def adapter_forward(rows_in, weight, down, up):
    inner = product("sti,sir->str", rows_in, down).astype(BF)
    mapped = product("sti,io->sto", rows_in, weight) + ADAPTER_SCALING * product(
        "str,sro->sto", inner, up
    )
    return (mapped, inner)


def adapter_back(rows_in, inner, weight, down, up, gradient):
    grad_up = ADAPTER_SCALING * product("str,sto->sro", inner, gradient)
    grad_inner = (ADAPTER_SCALING * product("sto,sro->str", gradient, up)).astype(BF)
    grad_down = product("sti,str->sir", rows_in, grad_inner)
    grad_in = product("sto,io->sti", gradient, weight) + product("str,sir->sti", grad_inner, down)
    return (grad_in, grad_down, grad_up)


def body(
    tokens,
    cotangent,
    doc_lengths,
    adapter_ids,
    query_weight,
    key_weight,
    value_weight,
    output_weight,
    up_weight,
    down_weight,
    attention_gain,
    feedforward_gain,
    position_gain,
    position_table,
    attention_down,
    attention_up,
    expand_down,
    expand_up,
    reduce_down,
    reduce_up,
):
    seqs, row_count, width = tokens.shape
    head_groups = lax.axis_size("head")
    head_index = lax.axis_index("head")
    seq_index = lax.axis_index("seq")
    by_rows = row_count >= HALF

    def chosen(stack, axis):
        return jnp.take(stack, adapter_ids, axis=axis).astype(BF)

    att_down = [chosen(attention_down[member], 0) for member in range(4)]
    att_up = [chosen(attention_up[member], 0) for member in range(4)]
    exp_down = chosen(expand_down, 0)
    exp_up = chosen(expand_up, 0)
    red_down = chosen(reduce_down, 0)
    red_up = chosen(reduce_up, 0)

    token_low = tokens.astype(BF)
    frozen = (query_weight, key_weight, value_weight)

    def columns(matrix):
        if by_rows:
            return matrix
        local = width // head_groups
        return lax.dynamic_slice_in_dim(matrix, head_index * local, local, matrix.ndim - 1)

    if by_rows:
        block_axes = ("seq", "head")
        block_index = seq_index * head_groups + head_index
        query_count = row_count
    else:
        block_axes = ("seq",)
        block_index = seq_index
        query_count = row_count * head_groups
    blocks = math.prod(lax.axis_size(axis) for axis in block_axes)

    def halo(array):
        before = shifted(array[:, query_count - HALF :], block_axes, 1)
        after = shifted(array[:, :HALF], block_axes, -1)
        return before, after

    if by_rows:
        before, after = halo(token_low)
        query_map, query_inner = adapter_forward(token_low, frozen[0], att_down[0], att_up[0])
        queries = query_map.astype(BF)
        rows_ext = jnp.concatenate([before, token_low, after], axis=1)
        inners = [query_inner]
        extended = []
        for member in (1, 2):
            mapped, inner = adapter_forward(rows_ext, frozen[member], att_down[member], att_up[member])
            extended.append(mapped.astype(BF))
            inners.append(inner)
        keys_ext, values_ext = extended
    else:
        projected = []
        inners = []
        for member in range(3):
            mapped, inner = adapter_forward(
                token_low, frozen[member], att_down[member], att_up[member]
            )
            projected.append(mapped.astype(BF))
            inners.append(inner)
        queries, keys, values = lax.all_to_all(
            jnp.stack(projected), "head", split_axis=3, concat_axis=2, tiled=True
        )
        keys_ext, values_ext = [
            jnp.concatenate([side[0], array, side[1]], axis=1)
            for array, side in ((keys, halo(keys)), (values, halo(values)))
        ]

    table_normed, table_inverse = norm_stats(position_table)
    table_low = (table_normed * position_gain).astype(BF)
    key_hot, query_hot, back_hot = (jnp.asarray(hot, BF) for hot in offset_tables())
    position_inners = []
    tables = []
    for member in range(2):
        inner = product("pi,sir->spr", table_low, att_down[member]).astype(BF)
        mapped = product("pi,io->po", table_low, columns(frozen[member]))[
            None
        ] + ADAPTER_SCALING * product("spr,sro->spo", inner, columns(att_up[member]))
        position_inners.append(inner)
        tables.append(mapped.astype(BF))
    key_rel = product("cp,spo->sco", key_hot, tables[1]).astype(BF)
    query_rel = product("cp,spo->sco", query_hot, tables[0]).astype(BF)
    query_back = product("cp,spo->sco", back_hot, tables[0]).astype(BF)

    key_places = block_index * query_count - HALF + jnp.arange(query_count + 2 * HALF, dtype=jnp.int32)
    key_segments = segment_ids(doc_lengths, key_places)
    inside = (key_places >= 0) & (key_places < query_count * blocks)
    key_segments = jnp.where(inside[None, :], key_segments, DOCS)
    query_segments = key_segments[:, HALF : HALF + query_count]
    slot = jnp.arange(TILE, dtype=jnp.int32) % HEAD_DIM
    query_seg = (slot == query_segments[..., None]).astype(BF)
    open_slot = (slot == key_segments[..., None]) & (key_segments[..., None] < DOCS)
    key_bias = jnp.where(open_slot | (slot > DOCS), 0.0, NEGATIVE).astype(BF)

    context, probs, context_wide, inverse_total = attention_forward(
        queries, keys_ext, values_ext, key_rel, query_rel, query_seg, key_bias
    )
    if by_rows:
        context_rows = context
    else:
        context_rows = lax.all_to_all(context, "head", split_axis=1, concat_axis=2, tiled=True)

    attended, inner_out = adapter_forward(context_rows, output_weight, att_down[3], att_up[3])
    normed_one, inverse_one = norm_stats(tokens + attended)
    hidden = normed_one * attention_gain
    hidden_low = hidden.astype(BF)
    pre_act, inner_up = adapter_forward(hidden_low, up_weight, exp_down, exp_up)
    act_low = jax.nn.gelu(pre_act, approximate=False).astype(BF)
    branch, inner_down = adapter_forward(act_low, down_weight, red_down, red_up)
    normed_two, inverse_two = norm_stats(hidden + branch)
    layer_output = normed_two * feedforward_gain
    grad_two = norm_back(normed_two, inverse_two, feedforward_gain, cotangent)
    grad_act, grad_red_down, grad_red_up = adapter_back(
        act_low, inner_down, down_weight, red_down, red_up, grad_two.astype(BF)
    )
    gelu_pull = jax.vjp(partial(jax.nn.gelu, approximate=False), pre_act)[1]
    grad_pre = gelu_pull(grad_act.astype(BF).astype(F32))[0].astype(BF)
    grad_hidden, grad_exp_down, grad_exp_up = adapter_back(
        hidden_low, inner_up, up_weight, exp_down, exp_up, grad_pre
    )
    grad_one = norm_back(normed_one, inverse_one, attention_gain, grad_hidden + grad_two)
    grad_context, grad_out_down, grad_out_up = adapter_back(
        context_rows, inner_out, output_weight, att_down[3], att_up[3], grad_one.astype(BF)
    )
    grad_context = grad_context.astype(BF)
    if not by_rows:
        grad_context = lax.all_to_all(grad_context, "head", split_axis=2, concat_axis=1, tiled=True)

    grad_q, grad_k, grad_v, grad_key_rel, grad_query_rel = attention_backward(
        queries,
        keys_ext,
        values_ext,
        key_rel,
        query_back,
        probs,
        grad_context,
        context_wide,
        inverse_total,
    )
    own = slice(HALF, HALF + query_count)

    def fold(array):
        from_above = shifted(array[:, :HALF].astype(BF), block_axes, -1).astype(F32)
        from_below = shifted(array[:, HALF + query_count :].astype(BF), block_axes, 1).astype(F32)
        total = array[:, own].astype(F32)
        if query_count == HALF:
            return total + from_above + from_below
        total = total.at[:, query_count - HALF :].add(from_above)
        return total.at[:, :HALF].add(from_below)

    down_grads = []
    up_grads = []
    if by_rows:
        grad_in, grad_dn, grad_upper = adapter_back(
            token_low, inners[0], frozen[0], att_down[0], att_up[0], grad_q
        )
        input_grad = grad_one + grad_in
        down_grads.append(grad_dn)
        up_grads.append(grad_upper)
        grad_rows = 0.0
        for member, gradient in ((1, grad_k), (2, grad_v)):
            grad_in, grad_dn, grad_upper = adapter_back(
                rows_ext, inners[member], frozen[member], att_down[member], att_up[member], gradient
            )
            grad_rows = grad_rows + grad_in
            down_grads.append(grad_dn)
            up_grads.append(grad_upper)
        input_grad = input_grad + fold(grad_rows)
    else:
        grad_qkv = jnp.stack([grad_q, fold(grad_k).astype(BF), fold(grad_v).astype(BF)])
        grad_qkv = lax.all_to_all(grad_qkv, "head", split_axis=2, concat_axis=3, tiled=True)
        input_grad = grad_one
        for member in range(3):
            grad_in, grad_dn, grad_upper = adapter_back(
                token_low,
                inners[member],
                frozen[member],
                att_down[member],
                att_up[member],
                grad_qkv[member],
            )
            input_grad = input_grad + grad_in
            down_grads.append(grad_dn)
            up_grads.append(grad_upper)
    down_grads.append(grad_out_down)
    up_grads.append(grad_out_up)

    position_grads = (
        split_product("cb,soc->sbo", back_hot, grad_query_rel),
        split_product("cb,soc->sbo", key_hot, grad_key_rel),
    )
    grad_table_low = jnp.zeros(position_table.shape, F32)
    for member in range(2):
        gradient = position_grads[member].astype(BF)
        up = columns(att_up[member])
        grad_columns = ADAPTER_SCALING * product("spr,spo->sro", position_inners[member], gradient)
        grad_inner = (ADAPTER_SCALING * product("spo,sro->spr", gradient, up)).astype(BF)
        grad_table_low = (
            grad_table_low
            + product("spo,io->pi", gradient, columns(frozen[member]))
            + product("spr,sir->pi", grad_inner, att_down[member])
        )
        down_grads[member] = down_grads[member] + product("pi,spr->sir", table_low, grad_inner)
        if not by_rows:
            grad_columns = lax.dynamic_update_slice_in_dim(
                jnp.zeros_like(up_grads[member]),
                grad_columns,
                head_index * (width // head_groups),
                2,
            )
        up_grads[member] = up_grads[member] + grad_columns
    table_grad = norm_back(table_normed, table_inverse, position_gain, grad_table_low)

    def reduced(parts):
        totals = lax.psum(parts, ("seq", "head"))
        totals = lax.all_gather(totals, "batch", axis=0, tiled=True)
        ids = lax.all_gather(adapter_ids, "batch", axis=0, tiled=True)
        count = ADAPTERS // head_groups
        slots = head_index * count + jnp.arange(count, dtype=jnp.int32)
        select = (ids[:, None] == slots[None, :]).astype(F32)

        def spread(array):
            shape = (array.shape[0], 1) + (1,) * (array.ndim - 1)
            return jnp.sum(
                select.reshape(select.shape + (1,) * (array.ndim - 1)) * array[:, None], axis=0
            )

        return [spread(array) for array in totals]

    early = reduced([grad_exp_down, grad_exp_up, grad_red_down, grad_red_up])
    late = reduced([jnp.stack(down_grads, axis=1), jnp.stack(up_grads, axis=1)])
    table_total = lax.psum(table_grad, ("seq", "batch"))
    table_total = lax.psum_scatter(table_total, "head", scatter_dimension=0, tiled=True)
    return (
        layer_output,
        input_grad,
        table_total,
        jnp.swapaxes(late[0], 0, 1),
        jnp.swapaxes(late[1], 0, 1),
        early[0],
        early[1],
        early[2],
        early[3],
    )


def solution(mesh):
    rows = P("batch", ("seq", "head"), None)
    return jax.shard_map(
        body,
        mesh=mesh,
        in_specs=(rows, rows, P("batch", None), P("batch")) + (P(),) * 16,
        out_specs=(
            rows,
            rows,
            P("head", None),
            P(None, "head", None, None),
            P(None, "head", None, None),
            P("head", None, None),
            P("head", None, None),
            P("head", None, None),
            P("head", None, None),
        ),
        check_vma=False,
    )
```

time: 3700 us -> 609 us (0.16)
  local copies, waits for them, and re-layouts: 2490 us -> 12.4 us
  matrix products: 540 us -> 195 us
  other arithmetic: 214 us -> 23.7 us
  waiting for transfers between devices: 389 us -> 219 us
  Pallas kernels: 0 us -> 105 us
    unnamed x239 -> x142, local copies, waits for them, and re-layouts: 1470 us -> 9.04 us
    reshape x5 -> x0, local copies, waits for them, and re-layouts: 485 us -> none  [the longest x4 481 us: skew_rows(): padded.reshape(head_count, row_count * (width + 1))[:, :row_count * width]]
    dot_general x80 -> x70, matrix products: 493 us -> 195 us  [product(): jnp.einsum(pattern, left_side, right_side, preferred_element_type=F32)]
    pad x4 -> x0, local copies, waits for them, and re-layouts: 233 us -> none  [the longest x2 133 us: skew_rows(): padded.reshape(head_count, row_count * (width + 1))[:, :row_count * width]]
    slice x16 -> x1, local copies, waits for them, and re-layouts: 204 us -> 1.48 us  [fold(): from_above = shifted(array[:, :HALF].astype(BF), block_axes, -1).astype(F32)]
    reduce_scatter x5 -> x1, waiting for transfers between devices: 133 us -> 0.01 us  [body(): lax.psum_scatter(table_total, 'head', scatter_dimension=0, tiled=True)]
    pallas_call x0 -> x2, Pallas kernels: none -> 105 us  [the longest x1 53.9 us: attention_forward(): pl.pallas_call(forward_kernel, grid=(n, pairs), in_specs=[col(rq), col(rk...]
    unnamed x4 -> x2, other arithmetic: 92.3 us -> 0.01 us
  transfers between devices with their start and end apart: 15 -> 7, of which waited for: 11 -> 6; matrix products, arithmetic and copies ran while one was open for 13% -> 13% of each run, Pallas kernels for 0% -> 0%
where the time goes in v1:
time: 609 us; the launch traced here: 602 us
  waiting for transfers between devices  219 us (36%)
  matrix products  195 us (32%)
  Pallas kernels  105 us (17%)
  other arithmetic  23.7 us (4%)
  between operations  17.1 us (3%)
  blocking collectives  14.7 us (2%)
  starting transfers between devices  14 us (2%)
  local copies, waits for them, and re-layouts  12.4 us (2%)
    dot_general x70, matrix products, product(): jnp.einsum(pattern, left_side, right_side, preferred_element_type=F32)  195 us
    psum x1, waiting for transfers between devices, body(): table_total = lax.psum(table_grad, ('seq', 'batch'))  87.2 us
    psum x1, waiting for transfers between devices, reduced(): totals = lax.psum(parts, ('seq', 'head'))  74 us
    ppermute x4, waiting for transfers between devices, shifted(): lax.ppermute(value, axes, [(source, source + steps) for source in range(i...  58.1 us
    pallas_call x1, Pallas kernels, attention_forward(): pl.pallas_call(forward_kernel, grid=(n, pairs), in_specs=[col(rq), col(rk...  53.9 us
    pallas_call x1, Pallas kernels, attention_backward(): pl.pallas_call(backward_kernel, grid=(n, pairs), in_specs=[col(rq), col(r...  51.3 us
    ppermute x4, starting transfers between devices, shifted(): lax.ppermute(value, axes, [(source, source + steps) for source in range(i...  13.9 us
    all_gather x6, blocking collectives, reduced(): totals = lax.all_gather(totals, 'batch', axis=0, tiled=True)  12.9 us
  transfers between devices with their start and end apart: 7, of which 6 were waited for; matrix products, arithmetic and copies ran while one was open for 13% of the time, Pallas kernels for 0%

profile of v1, /device:TPU:0, one launch (start us, length us, event | category | flops | bytes accessed | tf_op | source)
XLA Modules:
  0.0 601.6 jit_solution(6230581431100786632)
XLA Ops:
  8.1 2.9 convert_element_type.290
  11.0 5.8 collective-permute-start
  19.7 2.0 reduce_sum.185
  21.7 2.1 multiply_reduce_fusion.9
  24.2 2.2 convolution_convert_fusion.6
  26.8 2.6 fusion.213
  29.4 4.0 fusion.117
  34.8 2.6 fusion.212
  37.7 2.2 add_convert_fusion.6
  39.9 2.6 convert_bitcast_fusion.1.pq_ref
  42.5 2.7 convert_bitcast_fusion.pq_ref
  45.8 5.0 convert_bitcast_fusion.2.pk_ref
  50.8 1.5 select_convert_fusion.kbias_ref
  52.4 8.6 %collective-permute-done = bf16[1,512,1024]{2,1,0:T(8,128)(2,1)} collective-permute-done((bf16[1,512,1024]{2,1,0:T(8,128)(2,1)}, bf16[1,512,1024]{2,1,0:T(8,128)(2,1)}, u32[]{:S(2)}, u32[]{:S(2)}) %collective-permute-start) | collective-permute-done | bytes 1048608 | tf_op jit(solution)/shard_map/ppermute | solution.py:293
  61.0 1.9 collective-permute-done.1
  62.9 2.8 convolution_convert_fusion.1
  66.7 2.8 convolution_convert_fusion
  69.5 1.8 fusion.151
  71.3 7.3 %fusion.14.k_ref = bf16[1,1536,1024]{2,1,0:T(8,128)(2,1)} fusion(f32[1536,1024]{1,0:T(8,128)S(1)} %fusion.211, bf16[1024,1024]{1,0:T(8,128)(2,1)S(1)} %copy-done, bf16[1,512,1024]{2,1,0:T(8,128)(2,1)} %collective-permute-done.1, bf16[1,512,1024]{2,1,0:T(8,128)(2,1)} %convert_element_type.290, bf16[1,512,1024]{2,1,0:T(8,128)(2,1)} %collective-permute-done), kind=kOutput, calls=%fused_computation.35 | convolution fusion | flops 3235381248 | bytes 14680064 | tf_op jit(solution)/shard_map/sti,io->sto/dot_general | solution.py:326
  78.6 7.1 %fusion.15.v_ref = bf16[1,1536,1024]{2,1,0:T(8,128)(2,1)} fusion(f32[1536,1024]{1,0:T(8,128)S(1)} %fusion.151, bf16[1024,1024]{1,0:T(8,128)(2,1)S(1)} %copy-done.54, bf16[1,512,1024]{2,1,0:T(8,128)(2,1)} %collective-permute-done.1, bf16[1,512,1024]{2,1,0:T(8,128)(2,1)} %convert_element_type.290, bf16[1,512,1024]{2,1,0:T(8,128)(2,1)} %collective-permute-done), kind=kOutput, calls=%fused_computation.36 | convolution fusion | flops 3235381248 | bytes 14680064 | tf_op jit(solution)/shard_map/sti,io->sto/dot_general | solution.py:326
  85.7 53.9 %attention_forward.1 = (bf16[1,512,1024]{2,1,0:T(8,128)(2,1)S(1)}, bf16[1,16,2,256,1280]{4,3,2,1,0:T(8,128)(2,1)}, f32[1,512,1024]{2,1,0:T(8,128)S(1)}, f32[1,16,512,128]{3,2,1,0:T(8,128)}) custom-call(bf16[1,512,1024]{2,1,0:T(8,128)(2,1)S(1)} %fusion.58.q_ref, bf16[1,1536,1024]{2,1,0:T(8,128)(2,1)} %fusion.14.k_ref, bf16[1,1536,1024]{2,1,0:T(8,128)(2,1)} %fusion.15.v_ref, ...), custom_call_target="tpu_custom_call" | custom-call | tf_op jit(solution)/shard_map/attention_forward/pallas_call | solution.py:144
  140.9 1.9 convolution_convert_fusion.3
  145.2 6.7 %fusion.214 = f32[512,4096]{1,0:T(8,128)} fusion(bf16[512,1024]{1,0:T(8,128)(2,1)S(1)} %fusion.97, bf16[1024,4096]{1,0:T(8,128)(2,1)S(1)} %bitcast.395), kind=kOutput, calls=%fused_computation.289 | convolution fusion | flops 4294967296 | bytes 17825792 | tf_op jit(solution)/shard_map/sti,io->sto/dot_general | solution.py:326
  153.1 23.6 %multiply_convert_fusion = (bf16[512,4096]{1,0:T(8,128)(2,1)S(1)}, f32[512,4096]{1,0:T(8,128)}, f32[512,4096]{1,0:T(8,128)}) fusion(f32[512,4096]{1,0:T(8,128)} %fusion.214, bf16[512,16]{0,1:T(8,128)(2,1)S(1)} %convolution_convert_fusion.2, f32[8,16,4096]{2,1,0:T(8,128)} %param.44, s32[]{:T(128)} %bitcast.3, pred[]{:T(512)} %bitcast.1), kind=kOutput, calls=%fused_computation.12 | convolution fusion | flops 207683584 | bytes 29508608 | tf_op jit(solution)/shard_map/str,sro->sto/dot_general | solution.py:326
  176.7 4.5 fusion.215
  181.3 2.1 convolution_convert_fusion.7
  183.4 1.8 fusion.199
  186.3 2.0 subtract_multiply_fusion.2
  190.4 10.4 %fusion.109 = f32[512,4096]{1,0:T(8,128)} fusion(bf16[4096,1024]{1,0:T(8,128)(2,1)} %param.36, f32[1,512,1024]{2,1,0:T(8,128)S(1)} %get-tuple-element.100), kind=kOutput, calls=%fused_computation.161 | convolution fusion | flops 4295491584 | bytes 18874368 | tf_op jit(solution)/shard_map/sto,io->sti/dot_general | solution.py:326
  202.2 10.4 %fusion.5 = bf16[512,4096]{1,0:T(8,128)(2,1)S(1)} fusion(f32[512,4096]{1,0:T(8,128)} %get-tuple-element.95, f32[512,4096]{1,0:T(8,128)} %get-tuple-element.112, f32[512,4096]{1,0:T(8,128)} %fusion.109, bf16[512,16]{0,1:T(8,128)(2,1)S(1)} %fusion.89, f32[8,4096,16]{1,2,0:T(8,128)} %param.45, s32[]{:T(128)} %bitcast.3, pred[]{:T(512)} %bitcast.1), kind=kOutput, calls=%fused_computation.8 | convolution fusion | flops 102825984 | bytes 29508608 | tf_op jit(solution)/shard_map/str,sir->sti/dot_general | solution.py:326
  212.6 7.0 %fusion.216 = f32[512,1024]{1,0:T(8,128)S(1)} fusion(bf16[512,4096]{1,0:T(8,128)(2,1)S(1)} %fusion.5, bf16[1024,4096]{1,0:T(8,128)(2,1)} %param.35), kind=kOutput, calls=%fused_computation.291 | convolution fusion | flops 4294967296 | bytes 14680064 | tf_op jit(solution)/shard_map/sto,io->sti/dot_general | solution.py:326
  219.6 2.1 fusion.94
  221.7 1.9 fusion.195
  227.9 2.2 fusion.59.g_ref
  230.1 51.3 %attention_backward.1 = (bf16[1,512,1024]{2,1,0:T(8,128)(2,1)}, bf16[1,1536,1024]{2,1,0:T(8,128)(2,1)}, bf16[1,1536,1024]{2,1,0:T(8,128)(2,1)}, f32[1,1024,1024]{2,1,0:T(8,128)}, f32[1,1024,1024]{2,1,0:T(8,128)}) custom-call(bf16[1,512,1024]{2,1,0:T(8,128)(2,1)} %copy-done.1, bf16[1,1536,1024]{2,1,0:T(8,128)(2,1)} %fusion.14.k_ref, ...), custom_call_target="tpu_custom_call" | custom-call | tf_op jit(solution)/shard_map/attention_backward/pallas_call | solution.py:267
  281.4 1.5 fusion.98
  282.9 1.6 fusion.91
  284.5 3.9 fusion.48
  292.2 1.8 fusion.34
  304.2 1.6 convolution_bitcast_fusion.7
  307.6 3.1 fusion.194
  311.5 2.5 convolution_bitcast_fusion.3
  314.0 2.4 fusion.82
  317.2 4.1 subtract_multiply_fusion
  321.3 4.5 fusion.202
  325.8 5.4 fusion.20
  331.3 5.6 fusion.26
  336.9 7.5 %fusion.200 = (bf16[1,1536,1024]{2,1,0:T(8,128)(2,1)S(1)}, f32[1,1536,1024]{2,1,0:T(8,128)}) fusion(f32[1536,1024]{1,0:T(8,128)S(1)} %copy-done.16, bf16[1536,16]{0,1:T(8,128)(2,1)S(1)} %fusion.34, bf16[8,1024,16]{1,2,0:T(8,128)(2,1)} %get-tuple-element.109, s32[]{:T(128)} %bitcast.3, pred[]{:T(512)} %bitcast.1, f32[1536,1024]{1,0:T(8,128)S(1)} %fusion.26, ...), kind=kOutput, calls=%fused_computation.283 | convolution fusion | flops 56639488 | bytes 28394496 | tf_op jit(solution)/shard_map/str,sir->sti/dot_general | solution.py:326
  344.4 1.5 fusion.197
  347.1 5.5 collective-permute-start.3
  354.0 1.8 all-reduce
  355.9 3.0 fusion.101
  358.9 27.9 %collective-permute-done.2 = bf16[1,512,1024]{2,1,0:T(8,128)(2,1)} collective-permute-done((bf16[1,512,1024]{2,1,0:T(8,128)(2,1)}, bf16[1,512,1024]{2,1,0:T(8,128)(2,1)}, u32[]{:S(2)}, u32[]{:S(2)}) %collective-permute-start.2) | collective-permute-done | bytes 1048608 | tf_op jit(solution)/shard_map/ppermute | solution.py:293
  386.8 19.7 %collective-permute-done.3 = bf16[1,512,1024]{2,1,0:T(8,128)(2,1)} collective-permute-done((bf16[1,512,1024]{2,1,0:T(8,128)(2,1)}, bf16[1,512,1024]{2,1,0:T(8,128)(2,1)}, u32[]{:S(2)}, u32[]{:S(2)}) %collective-permute-start.3) | collective-permute-done | bytes 1048608 | tf_op jit(solution)/shard_map/ppermute | solution.py:293
  406.5 4.3 fusion.47
  410.8 74.0 %all-reduce.7.cloned.1.call-done = (f32[1,4,1024,16]{2,3,1,0:T(8,128)}, f32[1,4,16,1024]{3,2,1,0:T(8,128)}, f32[1,1024,16]{1,2,0:T(8,128)}, f32[1,16,4096]{2,1,0...) async-done(((f32[1,4,1024,16]{2,3,1,0:T(8,128)}, f32[1,4,16,1024]{3,2,1,0:T(8,128)}, f32[1,1024,16]{1,2,0:T(8,128)}, f32[1,16,4096]{2,1,0:T(8,128)}, ...) | async-done | bytes 1179664 | tf_op jit(solution)/shard_map/psum | solution.py:603
  484.8 2.5 all_gather.24
  488.6 2.3 all_gather.23
  492.2 1.9 all_gather.28
  494.1 1.9 all_gather.25
  496.8 2.2 all_gather.27
  499.8 2.2 all_gather.26
  504.4 87.2 %all-reduce.5.cloned.1.call-done = f32[256,1024]{1,0:T(8,128)} async-done(((f32[256,1024]{1,0:T(8,128)}), f32[256,1024]{1,0:T(8,128)}) %all-reduce.5.cloned.1.call-update) | async-done | bytes 1048592 | tf_op jit(solution)/shard_map/psum | solution.py:620
  591.7 2.3 copy.61
  (223 shorter events, 46.7 us)
Async XLA Ops:
  8.0 26.7 %copy-start = (bf16[1024,1024]{1,0:T(8,128)(2,1)S(1)}, bf16[1024,1024]{1,0:T(8,128)(2,1)}, u32[]{:S(2)}) copy-start(bf16[1024,1024]{1,0:T(8,128)(2,1)} %param.32) | copy-start | bytes 6291460
  8.0 476.8 %all-reduce.7.cloned.1.call-start = ((), (), s32[]{:S(2)}) async-start(), calls=%async_computation.3 | async-start | bytes 2359296 | tf_op jit(solution)/shard_map/psum | solution.py:603
  8.1 10.7 %copy-start.24 = (f32[4,8,1024,16]{2,3,1,0:T(8,128)S(1)}, f32[4,8,1024,16]{2,3,1,0:T(8,128)}, u32[]{:S(2)}) copy-start(f32[4,8,1024,16]{2,3,1,0:T(8,128)} %param.41) | copy-start | bytes 6291460
  11.0 50.0 %collective-permute-start = (bf16[1,512,1024]{2,1,0:T(8,128)(2,1)}, bf16[1,512,1024]{2,1,0:T(8,128)(2,1)}, u32[]{:S(2)}, u32[]{:S(2)}) collective-permute-start(bf16[1,512,1024]{2,1,0:T(8,128)(2,1)} %convert_element_type.290), channel_id=1, source_target_pairs={{0,2},{2,4},{4,6},{6,8},{8,10},{10,12},{12,14},{14,16},{16,18},{18... | collective-permute-start | bytes 3145736 | tf_op jit(solution)/shard_map/ppermute | solution.py:293
  16.8 46.2 %collective-permute-start.1 = (bf16[1,512,1024]{2,1,0:T(8,128)(2,1)}, bf16[1,512,1024]{2,1,0:T(8,128)(2,1)}, u32[]{:S(2)}, u32[]{:S(2)}) collective-permute-start(bf16[1,512,1024]{2,1,0:T(8,128)(2,1)} %convert_element_type.290), channel_id=1, source_target_pairs={{2,0},{4,2},{6,4},{8,6},{10,8},{12,10},{14,12},{16,14},{18,16},{20... | collective-permute-start | bytes 3145736 | tf_op jit(solution)/shard_map/ppermute | solution.py:293
  18.7 5.1 copy-start.48
  19.7 6.7 %copy-start.21 = (bf16[8,1024,16]{1,2,0:T(8,128)(2,1)}, bf16[8,1024,16]{1,2,0:T(8,128)(2,1)S(1)}, u32[]{:S(2)}) copy-start(bf16[8,1024,16]{1,2,0:T(8,128)(2,1)S(1)} %get-tuple-element.108) | copy-start | bytes 786436
  19.7 14.7 %copy-start.26 = (bf16[8,1024,16]{1,2,0:T(8,128)(2,1)}, bf16[8,1024,16]{1,2,0:T(8,128)(2,1)S(1)}, u32[]{:S(2)}) copy-start(bf16[8,1024,16]{1,2,0:T(8,128)(2,1)S(1)} %get-tuple-element.107) | copy-start | bytes 786436
  21.6 2.2 copy-start.3
  21.7 4.7 copy-start.42
  23.8 3.0 copy-start.56
  23.8 5.6 copy-start.45
  24.2 10.5 %copy-start.7 = (bf16[512,1024]{1,0:T(8,128)(2,1)}, bf16[512,1024]{1,0:T(8,128)(2,1)S(1)}, u32[]{:S(2)}) copy-start(bf16[512,1024]{1,0:T(8,128)(2,1)S(1)} %multiply_convert_fusion.1) | copy-start | bytes 3145732
  26.4 18.8 %copy-start.36 = (bf16[16,512]{1,0:T(8,128)(2,1)}, bf16[16,512]{1,0:T(8,128)(2,1)S(1)}, u32[]{:S(2)}) copy-start(bf16[16,512]{1,0:T(8,128)(2,1)S(1)} %convolution_convert_fusion.6) | copy-start | bytes 49156
  26.8 10.9 %copy-start.34 = (bf16[512,16]{0,1:T(8,128)(2,1)}, bf16[512,16]{0,1:T(8,128)(2,1)S(1)}, u32[]{:S(2)}) copy-start(bf16[512,16]{0,1:T(8,128)(2,1)S(1)} %fusion.96) | copy-start | bytes 49156
  29.4 4.0 copy-start.25
  34.7 11.1 %copy-start.38 = (bf16[512,16]{0,1:T(8,128)(2,1)}, bf16[512,16]{0,1:T(8,128)(2,1)S(1)}, u32[]{:S(2)}) copy-start(bf16[512,16]{0,1:T(8,128)(2,1)S(1)} %fusion.95) | copy-start | bytes 49156
  34.8 2.6 copy-start.58
  37.5 2.4 copy-start.61
  37.7 7.5 %copy-start.19 = (bf16[16,1024]{1,0:T(8,128)(2,1)}, bf16[16,1024]{1,0:T(8,128)(2,1)S(1)}, u32[]{:S(2)}) copy-start(bf16[16,1024]{1,0:T(8,128)(2,1)S(1)} %get-tuple-element.119) | copy-start | bytes 98308
  37.7 28.0 %copy-start.22 = (bf16[16,1024]{1,0:T(8,128)(2,1)}, bf16[16,1024]{1,0:T(8,128)(2,1)S(1)}, u32[]{:S(2)}) copy-start(bf16[16,1024]{1,0:T(8,128)(2,1)S(1)} %get-tuple-element.120) | copy-start | bytes 98308
  39.9 2.6 copy-start.59
  42.5 2.7 copy-start.18
  45.7 40.1 %copy-start.1 = (bf16[1,512,1024]{2,1,0:T(8,128)(2,1)}, bf16[1,512,1024]{2,1,0:T(8,128)(2,1)S(1)}, u32[]{:S(2)}) copy-start(bf16[1,512,1024]{2,1,0:T(8,128)(2,1)S(1)} %fusion.58.q_ref) | copy-start | bytes 3145732
  71.3 7.3 %copy-start.54 = (bf16[1024,1024]{1,0:T(8,128)(2,1)S(1)}, bf16[1024,1024]{1,0:T(8,128)(2,1)}, u32[]{:S(2)}) copy-start(bf16[1024,1024]{1,0:T(8,128)(2,1)} %param.33) | copy-start | bytes 6291460
  85.7 53.9 %copy-start.52 = (bf16[1024,1024]{1,0:T(8,128)(2,1)S(1)}, bf16[1024,1024]{1,0:T(8,128)(2,1)}, u32[]{:S(2)}) copy-start(bf16[1024,1024]{1,0:T(8,128)(2,1)} %param.34) | copy-start | bytes 6291460
  139.6 3.3 copy-start.15
  139.6 5.5 slice-start.2
  142.9 2.3 slice-start.3
  145.2 6.7 %copy-start.12 = (bf16[512,1024]{1,0:T(8,128)(2,1)}, bf16[512,1024]{1,0:T(8,128)(2,1)S(1)}, u32[]{:S(2)}) copy-start(bf16[512,1024]{1,0:T(8,128)(2,1)S(1)} %fusion.97) | copy-start | bytes 3145732
  145.2 31.5 %slice-start = ((s8[8388608]{0:T(1024)(128)(4,1)}), s8[4194304]{0:T(1024)(128)(4,1)S(1)}, s32[]{:S(2)}) async-start(s8[8388608]{0:T(1024)(128)(4,1)} %bitcast.392), calls=%async_computation.4 | async-start | bytes 8388608
  153.1 23.6 %slice-start.1 = ((s8[8388608]{0:T(1024)(128)(4,1)}), s8[4194304]{0:T(1024)(128)(4,1)S(1)}, s32[]{:S(2)}) async-start(s8[8388608]{0:T(1024)(128)(4,1)} %bitcast.392), calls=%async_computation.5 | async-start | bytes 8388608
  183.4 2.2 copy-start.14
  183.4 2.2 copy-start.47
  225.2 2.4 copy-start.5
  230.1 51.3 %copy-start.37 = (bf16[16,512]{1,0:T(8,128)(2,1)S(1)}, bf16[16,512]{1,0:T(8,128)(2,1)}, u32[]{:S(2)}) copy-start(bf16[16,512]{1,0:T(8,128)(2,1)} %copy-done.36) | copy-start | bytes 49156
  230.1 52.8 %copy-start.20 = (bf16[16,1024]{1,0:T(8,128)(2,1)S(1)}, bf16[16,1024]{1,0:T(8,128)(2,1)}, u32[]{:S(2)}) copy-start(bf16[16,1024]{1,0:T(8,128)(2,1)} %copy-done.19) | copy-start | bytes 98308
  284.5 3.9 copy-start.51
  284.5 4.1 copy-start.62
  289.8 1.9 copy-start.9
  289.8 1.9 copy-start.33
  292.2 4.1 copy-start.60
  294.0 2.6 copy-start.50
  300.8 1.9 copy-start.11
  303.6 3.4 copy-start.8
  304.2 3.4 copy-start.4
  304.2 3.4 copy-start.43
  304.2 3.4 copy-start.46
  304.2 3.4 copy-start.49
  317.1 181.9 %reduce-scatter.2.cloned.1.call-start = ((), (), s32[]{:S(2)}) async-start(), calls=%async_computation.1 | async-start | bytes 3145728 | tf_op jit(solution)/shard_map/reduce_scatter | solution.py:621
  321.3 4.5 copy-start.10
  321.3 4.5 copy-start.55
  331.2 260.5 %all-reduce.5.cloned.1.call-start = ((), (), s32[]{:S(2)}) async-start(), calls=%async_computation.2 | async-start | bytes 2097152 | tf_op jit(solution)/shard_map/psum | solution.py:620
  331.3 5.6 copy-start.16
  344.4 8.3 %copy-start.63 = (u32[32]{0:T(128)S(1)}, u32[32]{0:T(128)}, u32[]{:S(2)}) copy-start(u32[32]{0:T(128)} %constant.303) | copy-start | bytes 388
  344.4 11.5 %copy-start.17 = (bf16[1,512,1024]{2,1,0:T(8,128)(2,1)S(1)}, bf16[1,512,1024]{2,1,0:T(8,128)(2,1)}, u32[]{:S(2)}) copy-start(bf16[1,512,1024]{2,1,0:T(8,128)(2,1)} %get-tuple-element.24) | copy-start | bytes 3145732
  345.9 41.0 %collective-permute-start.2 = (bf16[1,512,1024]{2,1,0:T(8,128)(2,1)}, bf16[1,512,1024]{2,1,0:T(8,128)(2,1)}, u32[]{:S(2)}, u32[]{:S(2)}) collective-permute-start(bf16[1,512,1024]{2,1,0:T(8,128)(2,1)} %get-tuple-element.98), channel_id=1, source_target_pairs={{2,0},{4,2},{6,4},{8,6},{10,8},{12,10},{14,12},{16,14},{18,16},{20... | collective-permute-start | bytes 3145736 | tf_op jit(solution)/shard_map/ppermute | solution.py:293
  347.1 59.4 %collective-permute-start.3 = (bf16[1,512,1024]{2,1,0:T(8,128)(2,1)}, bf16[1,512,1024]{2,1,0:T(8,128)(2,1)}, u32[]{:S(2)}, u32[]{:S(2)}) collective-permute-start(bf16[1,512,1024]{2,1,0:T(8,128)(2,1)} %get-tuple-element.99), channel_id=1, source_target_pairs={{0,2},{2,4},{4,6},{6,8},{8,10},{10,12},{12,14},{14,16},{16,18},{18... | collective-permute-start | bytes 3145736 | tf_op jit(solution)/shard_map/ppermute | solution.py:293
  355.9 50.6 %copy-start.6 = (f32[1,512,1024]{2,1,0:T(8,128)S(1)}, f32[1,512,1024]{2,1,0:T(8,128)}, u32[]{:S(2)}) copy-start(f32[1,512,1024]{2,1,0:T(8,128)} %copy-done.5) | copy-start | bytes 6291460
  484.8 3.8 copy-start.29
  487.6 4.7 copy-start.41
  487.6 6.6 %copy-start.40 = (f32[1,1024,16]{1,2,0:T(8,128)S(1)}, f32[1,1024,16]{1,2,0:T(8,128)}, u32[]{:S(2)}) copy-start(f32[1,1024,16]{1,2,0:T(8,128)} %get-tuple-element.90) | copy-start | bytes 196612
  488.6 8.2 %copy-start.28 = (f32[1,4096,16]{1,2,0:T(8,128)S(1)}, f32[1,4096,16]{1,2,0:T(8,128)}, u32[]{:S(2)}) copy-start(f32[1,4096,16]{1,2,0:T(8,128)} %get-tuple-element.92) | copy-start | bytes 786436
  490.9 8.9 %copy-start.27 = (f32[1,16,4096]{2,1,0:T(8,128)S(1)}, f32[1,16,4096]{2,1,0:T(8,128)}, u32[]{:S(2)}) copy-start(f32[1,16,4096]{2,1,0:T(8,128)} %get-tuple-element.91) | copy-start | bytes 786436
  (11 other events, 16.4 us)
Sparse Core Ops, SparseCore 0:
  317.3 167.4 all-reduce.6
Sparse Core Ops, SparseCore 1:
  331.3 62.8 reduce-scatter.1
  499.1 92.5 all-reduce.4
